TPU v7x, 32 devices: a whole 2x2x4 slice. The times are simulated.
32 devices in a mesh: rep: 16 (over z, y, core), shard: 2 (over x).
Axes of the slice: x: 2, y: 2, z: 4, core: 2. Of those that a mesh axis runs over, the one named last changes fastest.
Arguments:
- tokens: bfloat16 [32768, 576], P(('rep', 'shard')), may hold values from -6 to 6
- cotangent: bfloat16 [32768, 576], P(('rep', 'shard')), may hold values from -6 to 6
- lengths: int32 [32, 4], P(('rep', 'shard')), may hold values from 1 to 512, 1024 in all within a row
- w_query: bfloat16 [576, 576], P('shard'), may hold values from -0.25 to 0.25
- w_key: bfloat16 [576, 192], P('shard'), may hold values from -0.25 to 0.25
- w_value: bfloat16 [576, 192], P('shard'), may hold values from -0.25 to 0.25
- w_out: bfloat16 [576, 576], P('shard'), may hold values from -1 to 1
- attn_gain: bfloat16 [576], P('shard'), may hold values from 0.099609375 to 1.8984375
- w_gate: bfloat16 [576, 1536], P('shard'), may hold values from -0.25 to 0.25
- w_up: bfloat16 [576, 1536], P('shard'), may hold values from -0.25 to 0.25
- w_down: bfloat16 [1536, 576], P('shard'), may hold values from -0.21875 to 0.21875
- mlp_gain: bfloat16 [576], P('shard'), may hold values from 0.099609375 to 1.8984375
Outputs:
- output: bfloat16 [32768, 576], P(('rep', 'shard'))
- d_tokens: float32 [32768, 576], P(('rep', 'shard'))
- grad_query: float32 [576, 576], P('shard')
- grad_key: float32 [576, 192], P('shard')
- grad_value: float32 [576, 192], P('shard')
- grad_out: float32 [576, 576], P('shard')
- grad_attn_gain: float32 [576], P('shard')
- grad_gate: float32 [576, 1536], P('shard')
- grad_up: float32 [576, 1536], P('shard')
- grad_down: float32 [1536, 576], P('shard')
- grad_mlp_gain: float32 [576], P('shard')
Inputs may be any that keep to these rules, and one draw needn't show every extreme that they name: Each row of lengths sums to 1024, and one entry of every row is exactly 512.
All inputs are finite; a program needn't handle non-finite values.
Results may differ from a plain program's by a relative error of at most 0.015.
Values may be sent and summed in bfloat16 or wider, within the bound.
No kernel may reach another device: no remote copies, remote signals or barrier semaphores. Data moves between devices by JAX's collectives and lax.ppermute only.
A program may use at most 192 MiB of HBM per device.

v0:
```python
import functools

import jax
import jax.numpy as jnp
from jax import lax
from jax.experimental import pallas as pl
from jax.experimental.pallas import tpu as pltpu
from jax.sharding import PartitionSpec as P

H = 9
KVH = 3
HD = 64
MAXLEN = 512
EPS = 1e-05
THETA = 100000.0
BLOCK = 256
STRIP = 128
GROUPS = H // KVH
GQ = GROUPS * HD
GD = GQ + 2 * HD
SCALE = HD ** (-0.5)
F32 = jnp.float32
BF16 = jnp.bfloat16
MIB = 1024 * 1024


def dot_nn(left, right):
    return lax.dot_general(left, right, (((1,), (0,)), ((), ())), preferred_element_type=F32)


def dot_nt(left, right):
    return lax.dot_general(left, right, (((1,), (1,)), ((), ())), preferred_element_type=F32)


def dot_tn(left, right):
    return lax.dot_general(left, right, (((0,), (0,)), ((), ())), preferred_element_type=F32)


def put_rows(full, own, got_a, got_b, shard, core):
    rows = own.shape[0]
    half = rows // 2
    full[pl.ds(pl.multiple_of(shard * rows, 16), rows), :] = own[...]
    other = (1 - shard) * rows
    full[pl.ds(pl.multiple_of(other + core * half, 16), half), :] = got_a[...]
    full[pl.ds(pl.multiple_of(other + (1 - core) * half, 16), half), :] = got_b[...]


def pack_first_kernel(wq, wk, wv, attn_gain, mlp_gain, packed):
    core = lax.axis_index("rep") % 2
    rows, width = wq.shape
    part = rows // 2
    half = pl.ds(pl.multiple_of(core * part, 16), part)
    packed[:part, :width] = wq[half, :]
    packed[:part, width : width + KVH * HD] = wk[half, :]
    packed[:part, width + KVH * HD :] = wv[half, :]
    row = lax.broadcasted_iota(jnp.int32, (packed.shape[0] - part, rows), 0)
    first = attn_gain[...].astype(F32).reshape(1, rows)
    second = mlp_gain[...].astype(F32).reshape(1, rows)
    packed[part:, :rows] = jnp.where(row == 0, first, jnp.where(row == 1, second, 0.0)).astype(BF16)


def pack_rest_kernel(ids, wg, wu, wd, wo, packed_0, packed_1):
    core = ids[1]
    rows = wg.shape[0]
    part = rows // 2
    lane = 128
    shift = wg.shape[1] // 2
    steps = packed_1.shape[1] // (6 * lane)
    first = shift // lane - steps
    half = pl.ds(pl.multiple_of(core * part, 16), part)
    for packed, begin, end in ((packed_0, 0, first), (packed_1, first, first + steps)):
        for step in range(begin, end):
            low = slice(step * lane, (step + 1) * lane)
            high = slice(shift + low.start, shift + low.stop)
            to = (step - begin) * 6 * lane
            for at, (source, columns) in enumerate(((wg, low), (wg, high), (wu, low), (wu, high))):
                packed[:, to + at * lane : to + (at + 1) * lane] = source[half, columns]
            for side in range(2):
                down = pl.ds(pl.multiple_of(core * rows + side * part, 16), part)
                packed[:, to + (4 + side) * lane : to + (5 + side) * lane] = wd[down, low]
    to = first * 6 * lane
    packed_0[:, to : to + wo.shape[1]] = wo[half, :]


def project_kernel(
    ids, tok, wq, wk, wv, packed, got_a, got_b, cos, sin,
    w_full, gains, normed, q_out, k_out, v_out,
):
    shard, core = ids[0], ids[1]
    rows = wq.shape[0]
    own = pl.ds(pl.multiple_of(shard * rows, 16), rows)
    part = rows // 2
    other = (1 - shard) * rows
    w_full[own, : wq.shape[1]] = wq[...]
    w_full[own, wq.shape[1] : wq.shape[1] + KVH * HD] = wk[...]
    w_full[own, wq.shape[1] + KVH * HD :] = wv[...]
    w_full[pl.ds(pl.multiple_of(other + core * part, 16), part), :] = got_a[:part, :]
    w_full[pl.ds(pl.multiple_of(other + (1 - core) * part, 16), part), :] = got_b[:part, :]
    lanes = (rows + 127) // 128 * 128
    gains[own, :] = packed[part:, :lanes].astype(F32).T[:rows, :8]
    gains[pl.ds(pl.multiple_of(other, 16), rows), :] = got_a[part:, :lanes].astype(F32).T[:rows, :8]
    width, count = tok.shape
    kv = KVH * HD
    half = HD // 2
    gain = gains[:, 0:1]
    for at in range(0, count, BLOCK):
        lanes = slice(at, at + BLOCK)
        x = tok[:, lanes].astype(F32)
        r = lax.rsqrt(jnp.mean(x * x, axis=0, keepdims=True) + EPS)
        normed[:, lanes] = (x * r * gain).astype(BF16)
    for at in range(0, count, BLOCK):
        lanes = slice(at, at + BLOCK)
        pre = dot_tn(w_full[...], normed[:, lanes])
        c = cos[:, lanes]
        s = sin[:, lanes]
        for head in range(H + KVH):
            row = head * HD
            a = pre[row : row + half]
            b = pre[row + half : row + HD]
            front = a * c - b * s
            back = b * c + a * s
            if head < H:
                q_out[row : row + half, lanes] = (front * SCALE).astype(BF16)
                q_out[row + half : row + HD, lanes] = (back * SCALE).astype(BF16)
            else:
                row -= width
                k_out[row : row + half, lanes] = front.astype(BF16)
                k_out[row + half : row + HD, lanes] = back.astype(BF16)
        v_out[:, lanes] = pre[width + kv :].astype(BF16)


def side_by_side(ref, lanes, rows=HD):
    return jnp.concatenate([ref[j * rows : (j + 1) * rows, lanes] for j in range(GROUPS)], axis=1)


def span_of(at, strips):
    return pl.ds(pl.multiple_of((at + 1) * BLOCK - strips * STRIP, STRIP), strips * STRIP)


def window(at, strips, starts):
    rows = lax.broadcasted_iota(jnp.int32, (strips * STRIP, GROUPS * BLOCK), 0)
    rows += span_of(at, strips).start
    columns = at * BLOCK + lax.broadcasted_iota(jnp.int32, (1, BLOCK), 1)
    starts = jnp.concatenate([starts] * GROUPS, axis=1)
    columns = jnp.concatenate([columns] * GROUPS, axis=1)
    return (rows >= starts) & (rows <= columns)


def reaches(count):
    own = BLOCK // STRIP
    return range(own, min(count // STRIP, own + (MAXLEN + STRIP - 2) // STRIP) + 1)


def attend_kernel(need, starts, q, k, v, att, att_low, lse, k_rows):
    count = q.shape[1]
    k_rows[...] = k[...].T

    @pl.loop(0, count // BLOCK)
    def _(at):
        lanes = pl.ds(pl.multiple_of(at * BLOCK, BLOCK), BLOCK)
        for strips in reaches(count):

            @pl.when(need[at] == strips)
            def _(strips=strips):
                ok = window(at, strips, starts[:, lanes])
                span = span_of(at, strips)
                scores = jnp.where(ok, dot_nn(k_rows[span, :], side_by_side(q, lanes)), -1e30)
                top = jnp.max(scores, axis=0, keepdims=True)
                e = jnp.exp(scores - top)
                total = jnp.sum(e, axis=0, keepdims=True)
                o = dot_nn(v[:, span], e.astype(BF16)) / total
                logs = top + jnp.log(total)
                for j in range(GROUPS):
                    rows = slice(j * HD, (j + 1) * HD)
                    one = slice(j * BLOCK, (j + 1) * BLOCK)
                    att[rows, lanes] = o[:, one]
                    att_low[rows, lanes] = o[:, one].astype(BF16)
                    lse[j : j + 1, lanes] = logs[:, one]


def place(target, shard, core, x, c, columns, value):
    away = jnp.where(core == c, 0, 2) + jnp.where(shard == x, 0, 1)
    target[away, :, columns] = value


def hidden_step(
    ids, cot, cot_rows, nm, nm_rows, acc_out, acc_e,
    wg_lo, wg_hi, wu_lo, wu_hi, wd_own, got_a, got_b, grads, wg, wu, wd, base,
):
    shard, core = ids[0], ids[1]
    width = cot.shape[0]
    rows, lane = wg_lo.shape
    half = rows // 2
    own = pl.ds(pl.multiple_of(shard * rows, 16), rows)
    other = (1 - shard) * rows
    at_a = pl.ds(pl.multiple_of(other + core * half, 16), half)
    at_b = pl.ds(pl.multiple_of(other + (1 - core) * half, 16), half)
    wg[own, :lane] = wg_lo[...]
    wg[own, lane:] = wg_hi[...]
    wu[own, :lane] = wu_lo[...]
    wu[own, lane:] = wu_hi[...]
    for at, got in ((at_a, got_a), (at_b, got_b)):
        wg[at, :] = got[:, : 2 * lane]
        wu[at, :] = got[:, 2 * lane : 4 * lane]
    for turn in range(2):

        @pl.when(shard == turn)
        def _(turn=turn):
            wd[:, turn * lane : (turn + 1) * lane] = wd_own[...]
            columns = slice((1 - turn) * lane, (2 - turn) * lane)
            for side in range(2):
                from_a = pl.ds(pl.multiple_of(core * rows + side * half, 16), half)
                from_b = pl.ds(pl.multiple_of((1 - core) * rows + side * half, 16), half)
                source = slice((4 + side) * lane, (5 + side) * lane)
                wd[from_a, columns] = got_a[:, source]
                wd[from_b, columns] = got_b[:, source]

    gate = dot_nn(nm_rows[...], wg[...])
    up = dot_nn(nm_rows[...], wu[...])
    dh = dot_nn(cot_rows[...], wd[...])
    sg = jax.nn.sigmoid(gate)
    sw = gate * sg
    hid = (sw * up).astype(BF16)
    dg = (dh * up * sg * (1.0 + gate * (1.0 - sg))).astype(BF16)
    du = (dh * sw).astype(BF16)
    acc_out[...] += dot_nt(wd[...], hid)
    acc_e[...] += dot_nt(wg[...], dg) + dot_nt(wu[...], du)
    g_gate = dot_nn(nm[...], dg).astype(BF16)
    g_up = dot_nn(nm[...], du).astype(BF16)
    g_down = dot_nn(cot[...], hid).astype(BF16)
    for x in range(2):
        for c in range(2):
            first = (2 * x + c) * half
            at_gate = pl.ds(pl.multiple_of(base, lane), 2 * lane)
            at_up = pl.ds(pl.multiple_of(base + 2 * lane, lane), 2 * lane)
            place(grads, shard, core, x, c, at_gate, g_gate[first : first + half])
            place(grads, shard, core, x, c, at_up, g_up[first : first + half])
            for side in range(2):
                first = c * rows + side * half
                value = g_down[first : first + half, x * lane : (x + 1) * lane]
                columns = pl.ds(pl.multiple_of(base + (4 + side) * lane, lane), lane)
                place(grads, shard, core, x, c, columns, value)


def middle_first_kernel(
    ids, tok, cot, att0, att1, att2, gains, wo_own, wo_a, wo_b,
    wg_lo, wg_hi, wu_lo, wu_hi, wd_own, got_a, got_b,
    mid_out, nm_out, acc_out, acc_e, wo_out, grads_0, grads_1, grads_2, grads_3,
    wg, wu, wd, nm_rows, cot_rows, mid, nm, wo, grads, sems, grad_sems,
):
    step = pl.program_id(0)
    block = 6 * wg_lo.shape[1]
    columns = pl.ds(pl.multiple_of(step * block, 128), block)
    outs = (grads_0, grads_1, grads_2, grads_3)
    leave = [
        pltpu.make_async_copy(grads.at[at, :, columns], out.at[:, columns], grad_sems.at[at])
        for at, out in enumerate(outs)
    ]
    copies = [
        pltpu.make_async_copy(source, target, sems.at[at])
        for at, (source, target) in enumerate(((mid, mid_out), (nm, nm_out), (wo, wo_out)))
    ]

    @pl.when(step == 0)
    def _():
        width = wo.shape[0]
        put_rows(wo, wo_own, wo_a.at[:, :width], wo_b.at[:, :width], ids[0], ids[1])
        copies[2].start()
        gain = gains[:, 1:2]
        att = jnp.concatenate([att0[...], att1[...], att2[...]], axis=0)
        mid[...] = tok[...].astype(F32) + dot_tn(wo[...], att)
        copies[0].start()
        for at in range(0, tok.shape[1], BLOCK):
            lanes = slice(at, at + BLOCK)
            m = mid[:, lanes]
            r = lax.rsqrt(jnp.mean(m * m, axis=0, keepdims=True) + EPS)
            part = (m * r * gain).astype(BF16)
            nm[:, lanes] = part
            nm_rows[lanes, :] = part.T
            cot_rows[lanes, :] = cot[:, lanes].T
        copies[1].start()
        acc_out[...] = jnp.zeros_like(acc_out)
        acc_e[...] = jnp.zeros_like(acc_e)

    hidden_step(
        ids, cot, cot_rows, nm, nm_rows, acc_out, acc_e,
        wg_lo, wg_hi, wu_lo, wu_hi, wd_own, got_a, got_b, grads, wg, wu, wd, step * block,
    )

    for copy in leave:
        copy.start()

    @pl.when(step == pl.num_programs(0) - 1)
    def _():
        for copy in copies:
            copy.wait()
        for at, out in enumerate(outs):
            pltpu.make_async_copy(grads.at[at], out, grad_sems.at[at]).wait()


def middle_second_kernel(
    ids, cot, nm, gains, att0, att1, att2, wo_in, mid_in, out_in, e_in,
    wg_lo, wg_hi, wu_lo, wu_hi, wd_own, got_a, got_b,
    out_out, d_mid_out, d_att_out, grads_0, grads_1, grads_2, grads_3,
    wg, wu, wd, nm_rows, cot_rows, acc_out, acc_e, att, wo, mid, out_first, e_first, out, d_att, grads,
    sems, grad_sems,
):
    step = pl.program_id(0)
    rows = att0.shape[0]
    arrive = [
        (att0, att.at[:rows, :]), (att1, att.at[rows : 2 * rows, :]), (att2, att.at[2 * rows :, :]),
        (wo_in, wo), (mid_in, mid), (out_in, out_first), (e_in, e_first),
    ]
    arrive = [pltpu.make_async_copy(*pair, sems.at[at]) for at, pair in enumerate(arrive)]
    leave = [(out, out_out), (mid, d_mid_out), (d_att, d_att_out)]
    leave = [pltpu.make_async_copy(*pair, sems.at[7 + at]) for at, pair in enumerate(leave)]
    grads_leave = [
        pltpu.make_async_copy(grads.at[at], out_at, grad_sems.at[at])
        for at, out_at in enumerate((grads_0, grads_1, grads_2, grads_3))
    ]

    @pl.when(step == 0)
    def _():
        for copy in arrive:
            copy.start()
        for at in range(0, cot.shape[1], BLOCK):
            lanes = slice(at, at + BLOCK)
            nm_rows[lanes, :] = nm[:, lanes].T
            cot_rows[lanes, :] = cot[:, lanes].T
        acc_out[...] = jnp.zeros_like(acc_out)
        acc_e[...] = jnp.zeros_like(acc_e)

    hidden_step(
        ids, cot, cot_rows, nm, nm_rows, acc_out, acc_e,
        wg_lo, wg_hi, wu_lo, wu_hi, wd_own, got_a, got_b, grads, wg, wu, wd,
        step * (6 * wg_lo.shape[1]),
    )

    @pl.when(step == pl.num_programs(0) - 1)
    def _():
        for copy in arrive:
            copy.wait()
        out[...] = (mid[...] + out_first[...] + acc_out[...]).astype(BF16)
        leave[0].start()
        gain = gains[:, 1:2]
        for at in range(0, cot.shape[1], BLOCK):
            lanes = slice(at, at + BLOCK)
            m = mid[:, lanes]
            r = lax.rsqrt(jnp.mean(m * m, axis=0, keepdims=True) + EPS)
            z = m * r
            e = (e_first[:, lanes] + acc_e[:, lanes]) * gain
            d_part = cot[:, lanes].astype(F32) + r * (e - z * jnp.mean(e * z, axis=0, keepdims=True))
            mid[:, lanes] = d_part
            nm_rows[lanes, :] = d_part.astype(BF16).T
        leave[1].start()
        low = nm_rows[...]
        d_att[...] = dot_nt(wo[...], low).astype(BF16)
        leave[2].start()
        value = dot_nn(att[...], low).astype(BF16)
        half = value.shape[0] // 4
        done = pl.num_programs(0) * 6 * wg_lo.shape[1]
        for x in range(2):
            for c in range(2):
                first = (2 * x + c) * half
                columns = slice(done, done + value.shape[1])
                place(grads, ids[0], ids[1], x, c, columns, value[first : first + half])
        for copy in grads_leave:
            copy.start()
        for copy in leave + grads_leave:
            copy.wait()


def attend_back_kernel(ids, need, starts, q, k, v, d_att, att, lse, cos, sin, normed, *refs):
    *refs, dk_acc, dv_acc, k_rows, v_rows = refs
    earlier = refs[:2] if len(refs) > 2 else []
    d_out, *targets = refs[len(earlier) :]
    count = q.shape[1]
    half = HD // 2
    k_rows[...] = k[...].T
    v_rows[...] = v[...].T
    dk_acc[...] = jnp.zeros_like(dk_acc)
    dv_acc[...] = jnp.zeros_like(dv_acc)

    @pl.loop(0, count // BLOCK)
    def _(at):
        lanes = pl.ds(pl.multiple_of(at * BLOCK, BLOCK), BLOCK)
        for strips in reaches(count):

            @pl.when(need[at] == strips)
            def _(strips=strips):
                ok = window(at, strips, starts[:, lanes])
                span = span_of(at, strips)
                c = cos[:, lanes]
                s = sin[:, lanes]
                q_part = side_by_side(q, lanes)
                d_part = side_by_side(d_att, lanes)
                scores = jnp.where(ok, dot_nn(k_rows[span, :], q_part), -1e30)
                probs = jnp.exp(scores - side_by_side(lse, lanes, 1))
                d_probs = dot_nn(v_rows[span, :], d_part)
                centre = jnp.sum(
                    d_part.astype(F32) * side_by_side(att, lanes), axis=0, keepdims=True
                )
                d_scores = (probs * (d_probs - centre)).astype(BF16)
                dq = dot_nn(k[:, span], d_scores) * SCALE
                for j in range(GROUPS):
                    one = slice(j * BLOCK, (j + 1) * BLOCK)
                    a = dq[:half, one]
                    b = dq[half:, one]
                    d_out[j * HD : j * HD + half, lanes] = (a * c + b * s).astype(BF16)
                    d_out[j * HD + half : (j + 1) * HD, lanes] = (b * c - a * s).astype(BF16)
                dk_acc[:, span] += dot_nt(q_part, d_scores)
                dv_acc[:, span] += dot_nt(d_part, probs.astype(BF16))
    a = dk_acc[:half, :]
    b = dk_acc[half:, :]
    d_out[GQ : GQ + half, :] = (a * cos[...] + b * sin[...]).astype(BF16)
    d_out[GQ + half : GQ + HD, :] = (b * cos[...] - a * sin[...]).astype(BF16)
    d_out[GQ + HD :, :] = dv_acc[...].astype(BF16)
    value = dot_nt(normed[...], d_out[...]).astype(BF16)
    quarter = value.shape[0] // 4
    for x in range(2):
        for c in range(2):
            first = (2 * x + c) * quarter
            part = value[first : first + quarter]
            if not earlier:
                place(targets[0], ids[0], ids[1], x, c, slice(None), part)
            for away, target in enumerate(targets if earlier else []):

                @pl.when((away // 2 == (ids[1] ^ c)) & (away % 2 == (ids[0] ^ x)))
                def _(target=target, part=part):
                    target[:, len(earlier) * GD :] = part

    for at, group in enumerate(earlier):
        for away, target in enumerate(targets):
            target[:, at * GD : (at + 1) * GD] = group[away]


def input_kernel(tok, d_mid, w_full, gains, d0, d1, d2, d_tok, d_all):
    width, count = tok.shape
    kv = KVH * HD
    for g, part in enumerate((d0, d1, d2)):
        d_all[g * GQ : (g + 1) * GQ, :] = part[:GQ, :]
        d_all[width + g * HD : width + (g + 1) * HD, :] = part[GQ : GQ + HD, :]
        d_all[width + kv + g * HD : width + kv + (g + 1) * HD, :] = part[GQ + HD :, :]
    gain = gains[:, 0:1]
    for at in range(0, count, BLOCK):
        lanes = slice(at, at + BLOCK)
        x = tok[:, lanes].astype(F32)
        r = lax.rsqrt(jnp.mean(x * x, axis=0, keepdims=True) + EPS)
        z = x * r
        e = dot_nn(w_full[...], d_all[:, lanes]) * gain
        d_tok[:, lanes] = d_mid[:, lanes] + r * (e - z * jnp.mean(e * z, axis=0, keepdims=True))


def row_of(column):
    rows = column.shape[0]
    lanes = (rows + 127) // 128 * 128
    wide = jnp.broadcast_to(column, (rows, 128))
    return jnp.concatenate([wide, jnp.zeros((lanes - rows, 128), F32)], axis=0).T[0, :rows]


def finish_hidden_kernel(
    ids, mine_1, got_1, mine_2, got_2, wg, wu, gains, gate, up, down, g_out, gain_out
):
    shard, core = ids[0], ids[1]
    rows, hidden = wg.shape
    half = rows // 2
    lane = 128
    steps = mine_1.shape[1] // (6 * lane)
    total_steps = hidden // 2 // lane
    sums = []
    for parts, side_of in (((mine_1, mine_2), core), ((got_1, got_2), 1 - core)):
        at = pl.ds(pl.multiple_of(side_of * half, 16), half)
        total = jnp.zeros((half, lane), F32)
        done = (total_steps - steps) * 6 * lane
        g_out[at, :] = parts[1][:, done : done + g_out.shape[1]].astype(F32)
        for turn, turn_steps in enumerate((steps, total_steps - steps)):
            for step in range(turn_steps):
                low = (turn * steps + step) * lane
                begin = step * 6 * lane
                for high in range(2):
                    columns = slice(high * hidden // 2 + low, high * hidden // 2 + low + lane)
                    g = parts[turn][:, begin + high * lane : begin + (high + 1) * lane].astype(F32)
                    u = parts[turn][:, begin + (2 + high) * lane : begin + (3 + high) * lane].astype(F32)
                    gate[at, columns] = g
                    up[at, columns] = u
                    total += wg[at, columns].astype(F32) * g + wu[at, columns].astype(F32) * u
                for side in range(2):
                    d = parts[turn][:, begin + (4 + side) * lane : begin + (5 + side) * lane]
                    to = pl.ds(pl.multiple_of(side_of * rows + side * half, 16), half)
                    down[to, low : low + lane] = d.astype(F32)
        sums.append((at, jnp.sum(total, axis=1, keepdims=True)))
    own = pl.ds(pl.multiple_of(shard * rows, 16), rows)
    gain = gains[own, 1:2]
    first = jnp.where(core == 0, sums[0][1], sums[1][1])
    second = jnp.where(core == 0, sums[1][1], sums[0][1])
    gain_out[...] = row_of(jnp.concatenate([first, second], axis=0) / gain)


def finish_last_kernel(ids, mine, got, wq, wk, wv, gains, g_query, g_key, g_value, gain_out):
    shard, core = ids[0], ids[1]
    rows = wq.shape[0]
    half = rows // 2
    sums = []
    for part, side_of in ((mine, core), (got, 1 - core)):
        at = pl.ds(pl.multiple_of(side_of * half, 16), half)
        total = jnp.zeros((half, 1), F32)
        for weight, grad, begin, length in (
            (wq, g_query, 0, GQ), (wk, g_key, GQ, HD), (wv, g_value, GQ + HD, HD)
        ):
            pieces = [
                part[:, g * GD + begin : g * GD + begin + length] for g in range(KVH)
            ]
            value = jnp.concatenate(pieces, axis=1).astype(F32)
            grad[at, :] = value
            total += jnp.sum(weight[at, :].astype(F32) * value, axis=1, keepdims=True)
        sums.append(total)
    own = pl.ds(pl.multiple_of(shard * rows, 16), rows)
    gain = gains[own, 0:1]
    first = jnp.where(core == 0, sums[0], sums[1])
    second = jnp.where(core == 0, sums[1], sums[0])
    gain_out[...] = row_of(jnp.concatenate([first, second], axis=0) / gain)


SMEM = pl.BlockSpec(memory_space=pltpu.SMEM)


def cost(microseconds):
    return pl.CostEstimate(flops=microseconds * 10**9, bytes_accessed=MIB, transcendentals=0)


def vmem(count):
    return [pl.BlockSpec(memory_space=pltpu.VMEM)] * count


def shape(dims, dtype):
    return jax.ShapeDtypeStruct(dims, dtype)


def after(value, *others):
    return lax.optimization_barrier((value, *others))[0]


class Stages:
    def __init__(self, stages):
        self.stages = stages
        self.now = next(stages)

    def step(self, marker=None):
        if not self.done():
            self.now = self.stages.send(marker)
        return self.marker()

    def done(self):
        return isinstance(self.now, tuple)

    def marker(self):
        return self.now[0] if self.done() else self.now


def shards(
    size, tokens, cotangent, lengths, w_query, w_key, w_value, w_out, attn_gain, w_gate, w_up, w_down,
    mlp_gain,
):
    count, width = tokens.shape
    kv = KVH * HD
    rows = w_query.shape[0]
    quarter = rows // 2
    hidden = w_gate.shape[1]
    part = w_down.shape[0]
    lane = 128
    all_steps = part // lane
    steps = (all_steps * 2 // 3, all_steps - all_steps * 2 // 3)
    chunk = 6 * lane
    rep = lax.axis_index("rep")
    shard = lax.axis_index("shard")
    core = rep % 2
    ids = jnp.stack([shard, core]).astype(jnp.int32)
    bits = size.bit_length() - 1

    def over_x(value):
        return lax.ppermute(value, "shard", [(0, 1), (1, 0)])

    def over_rep(value, bit):
        return lax.ppermute(value, "rep", [(i, i ^ (1 << bit)) for i in range(size)])

    def pick(value, axis, index, total):
        step = value.shape[axis] // total
        return lax.dynamic_slice_in_dim(value, index * step, step, axis)

    tok = tokens.T
    cot = cotangent.T
    down = w_down.T
    params = pltpu.CompilerParams(vmem_limit_bytes=56 * MIB)
    packed = pl.pallas_call(
        pack_first_kernel,
        out_shape=shape((quarter + 16, width + 2 * kv), BF16),
        in_specs=vmem(5),
        out_specs=pl.BlockSpec(memory_space=pltpu.VMEM),
        cost_estimate=cost(2),
        name="pack_first",
    )(w_query, w_key, w_value, attn_gain, mlp_gain)
    second, third = pl.pallas_call(
        pack_rest_kernel,
        out_shape=(
            shape((quarter, (steps[0] + 1) * chunk), BF16),
            shape((quarter, steps[1] * chunk), BF16),
        ),
        in_specs=[SMEM] + vmem(4),
        out_specs=vmem(2),
        compiler_params=params,
        cost_estimate=cost(3),
        name="pack_rest",
    )(after(ids, packed), w_gate, w_up, down, w_out)
    ends = jnp.cumsum(lengths[0], dtype=jnp.int32)
    begins = ends - lengths[0]
    row_ids = jnp.arange(count, dtype=jnp.int32)
    starts = jnp.max(jnp.where(row_ids[None, :] >= begins[:, None], begins[:, None], 0), axis=0)
    offset = (row_ids - starts).astype(F32)
    frequency = THETA ** (-2.0 * jnp.arange(HD // 2, dtype=F32) / HD)
    angles = frequency[:, None] * offset[None, :]
    cos = jnp.cos(angles)
    sin = jnp.sin(angles)
    at = jnp.arange(count // BLOCK, dtype=jnp.int32)
    first = jnp.max(jnp.where(at[:, None] * BLOCK >= begins[None, :], begins[None, :], 0), axis=1)
    need = (at + 1) * (BLOCK // STRIP) - first // STRIP
    starts = starts[None, :]

    first_a = after(over_x(packed), second, cos, sin, starts, need)
    first_b = over_rep(first_a, 0)
    second = after(second, first_a)

    w_full, gains, normed, q, k, v = pl.pallas_call(
        project_kernel,
        out_shape=(
            shape((width, width + 2 * kv), BF16),
            shape((width, 8), F32),
            shape((width, count), BF16),
            shape((width, count), BF16),
            shape((kv, count), BF16),
            shape((kv, count), BF16),
        ),
        in_specs=[SMEM] + vmem(9),
        out_specs=vmem(6),
        compiler_params=params,
        cost_estimate=cost(5),
        name="project",
    )(after(ids, second), tok, w_query, w_key, w_value, packed, first_a, first_b, cos, sin)

    def one(size_of, index):
        return pl.BlockSpec((size_of, count), lambda i: (index, 0))

    atts, lows, lses = [], [], []
    for g in range(KVH):
        att, low, lse = pl.pallas_call(
            attend_kernel,
            grid=(1,),
            out_shape=(shape((GQ, count), F32), shape((GQ, count), BF16), shape((8, count), F32)),
            in_specs=[SMEM, one(1, 0), one(GQ, g), one(HD, g), one(HD, g)],
            out_specs=(one(GQ, 0), one(GQ, 0), one(8, 0)),
            scratch_shapes=[pltpu.VMEM((count, HD), BF16)],
            compiler_params=params,
            cost_estimate=cost(7),
            name="attend",
        )(after(need, *lses[-1:]), starts, q, k, v)
        atts.append(att)
        lows.append(low)
        lses.append(lse)

    second_a = after(over_x(second), lses[-1])
    third = after(third, second_a)
    second_b = over_rep(second_a, 0)

    def whole(dims):
        return pl.BlockSpec(dims, lambda i: (0,) * len(dims))

    def hidden_specs(turn):
        begin = turn * steps[0]
        low = pl.BlockSpec((rows, lane), lambda i: (0, begin + i))
        high = pl.BlockSpec((rows, lane), lambda i: (0, all_steps + begin + i))
        return [
            low, high, low, high,
            pl.BlockSpec((width, lane), lambda i: (0, begin + i)),
            pl.BlockSpec((quarter, chunk), lambda i: (0, i)),
            pl.BlockSpec((quarter, chunk), lambda i: (0, i)),
        ]

    wide = whole((width, count))
    anywhere = pl.BlockSpec(memory_space=pl.ANY)
    att_specs = [whole((GQ, count))] * KVH
    grad_shapes = [
        shape((quarter, chunk * steps[0]), BF16),
        shape((quarter, chunk * (steps[1] + 1)), BF16),
    ]
    weight_scratch = [pltpu.VMEM((width, 2 * lane), BF16)] * 3 + [pltpu.VMEM((count, width), BF16)] * 2
    wo_spec = pl.BlockSpec((quarter, chunk), lambda i: (0, steps[0]))
    mid, nm, acc_out, acc_e, wo, *grads_1 = pl.pallas_call(
        middle_first_kernel,
        grid=(steps[0],),
        out_shape=(
            shape((width, count), F32),
            shape((width, count), BF16),
            shape((width, count), F32),
            shape((width, count), F32),
            shape((width, width), BF16),
            *[grad_shapes[0]] * 4,
        ),
        in_specs=[SMEM, wide, wide] + att_specs
        + [whole((width, 8)), whole((rows, width)), wo_spec, wo_spec] + hidden_specs(0),
        out_specs=(anywhere, anywhere, wide, wide, anywhere) + (anywhere,) * 4,
        scratch_shapes=weight_scratch
        + [
            pltpu.VMEM((width, count), F32),
            pltpu.VMEM((width, count), BF16),
            pltpu.VMEM((width, width), BF16),
            pltpu.VMEM((4, *grad_shapes[0].shape), BF16),
            pltpu.SemaphoreType.DMA((3,)),
            pltpu.SemaphoreType.DMA((4,)),
        ],
        compiler_params=params,
        cost_estimate=cost(18),
        name="middle_first",
    )(
        after(ids, third), tok, cot, *lows, gains, w_out, second_a, second_b,
        w_gate, w_gate, w_up, w_up, down, second_a, second_b,
    )

    def half_of(total, bit, axis):
        side = (rep >> bit) % 2
        return pick(total, axis, side, 2), pick(total, axis, 1 - side, 2)

    def join(total, got, bit, axis):
        side = (rep >> bit) % 2
        return jnp.where(
            side == 0,
            jnp.concatenate([total, got], axis=axis),
            jnp.concatenate([got, total], axis=axis),
        )

    def reduce_steps(stay, leave, send_stay, send_leave, cuts):
        def end(value, marker):
            return value if marker is None else after(value, marker)

        marker = yield send_leave
        sent = leave + end(over_rep(send_leave, 0), marker)
        stay = stay + over_rep(after(send_stay, sent), 0)
        marker = yield sent
        total = stay + end(over_x(sent), marker)
        done = []
        for bit in range(1, bits):
            if bit in cuts:
                stay, sent = half_of(total, bit, cuts[bit])
                done.append(bit)
            else:
                stay = sent = total
            marker = yield sent
            total = stay + end(over_rep(sent, bit), marker)
        for bit in reversed(done):
            marker = yield total
            total = join(total, end(over_rep(total, bit), marker), bit, cuts[bit])
        marker = yield total
        yield total, end(over_rep(total, 0), marker)

    third_a = after(over_x(third), mid)
    third_b = over_rep(third_a, 0)
    run_1 = Stages(reduce_steps(*grads_1[:3], after(grads_1[3], third_a), {1: 0, 2: 1}))
    out, d_mid, d_att, *grads_2 = pl.pallas_call(
        middle_second_kernel,
        grid=(steps[1],),
        out_shape=(
            shape((width, count), BF16),
            shape((width, count), F32),
            shape((width, count), BF16),
            *[grad_shapes[1]] * 4,
        ),
        in_specs=[SMEM, wide, wide, whole((width, 8))] + [anywhere] * (KVH + 4) + hidden_specs(1),
        out_specs=(
            *[anywhere] * 7,
        ),
        scratch_shapes=weight_scratch
        + [pltpu.VMEM((width, count), F32)] * 2
        + [pltpu.VMEM((width, count), BF16), pltpu.VMEM((width, width), BF16)]
        + [pltpu.VMEM((width, count), F32)] * 3
        + [pltpu.VMEM((width, count), BF16)] * 2
        + [pltpu.VMEM((4, *grad_shapes[1].shape), BF16)]
        + [pltpu.SemaphoreType.DMA((10,)), pltpu.SemaphoreType.DMA((4,))],
        compiler_params=params,
        cost_estimate=cost(18),
        name="middle_second",
    )(
        after(ids, run_1.step()), cot, nm, gains, *lows, wo, mid, acc_out, acc_e,
        w_gate, w_gate, w_up, w_up, down, third_a, third_b,
    )
    run_2 = Stages(reduce_steps(*grads_2, {1: 0, 2: 1}))
    sent = [run_1.step(d_mid), run_2.step()]

    d_parts, earlier = [], []
    for g in range(KVH):
        joined = earlier if g == KVH - 1 else []
        grads_to = [(quarter, GD * KVH)] * 4 if joined else [(4, quarter, GD)]
        d_part, *pair = pl.pallas_call(
            attend_back_kernel,
            grid=(1,),
            out_shape=(
                shape((GD, count), BF16),
                *[shape(dims, BF16) for dims in grads_to],
            ),
            in_specs=[
                SMEM, SMEM, one(1, 0), one(GQ, g), one(HD, g), one(HD, g), one(GQ, g), one(GQ, 0),
                one(8, 0), one(HD // 2, 0), one(HD // 2, 0), one(width, 0),
            ] + [whole(x.shape) for x in joined],
            out_specs=(one(GD, 0), *[whole(dims) for dims in grads_to]),
            scratch_shapes=[pltpu.VMEM((HD, count), F32)] * 2 + [pltpu.VMEM((count, HD), BF16)] * 2,
            compiler_params=params,
            cost_estimate=cost(10),
            name="attend_back",
        )(
            after(ids, *sent), need, starts, q, k, v, d_att, atts[g], lses[g],
            cos, sin, normed, *joined,
        )
        d_parts.append(d_part)
        earlier += pair
        sent = [run_1.step(d_part), run_2.step(d_part)]
    run_3 = Stages(reduce_steps(*pair[:3], after(pair[3], *sent), {1: 0}))
    sent.append(run_3.step())

    d_tok = pl.pallas_call(
        input_kernel,
        out_shape=shape((width, count), F32),
        in_specs=vmem(7),
        out_specs=pl.BlockSpec(memory_space=pltpu.VMEM),
        scratch_shapes=[pltpu.VMEM((width + 2 * kv, count), BF16)],
        compiler_params=params,
        cost_estimate=cost(7),
        name="input_grad",
    )(after(tok, *sent), d_mid, w_full, gains, *d_parts)

    sent = run_3.step(d_tok)
    run_1.step(after(d_tok, sent))
    run_2.step(after(d_tok, sent))
    sent = run_3.step()
    run_1.step(sent)
    run_2.step(sent)
    sent = run_3.step()
    run_1.step(sent)
    run_3.step()
    sent = run_3.step()
    while not (run_1.done() and run_2.done()):
        run_1.step(sent)
        run_2.step(sent)
    gain_shape = shape((rows,), F32)
    grad_gate, grad_up, grad_down, grad_out, grad_mlp_gain = pl.pallas_call(
        finish_hidden_kernel,
        out_shape=(
            shape((rows, hidden), F32), shape((rows, hidden), F32), shape((width, part), F32),
            shape((rows, width), F32), gain_shape,
        ),
        in_specs=[SMEM] + vmem(7),
        out_specs=vmem(5),
        compiler_params=params,
        cost_estimate=cost(5),
        name="finish_hidden",
    )(after(ids, sent), *run_1.now, *run_2.now, w_gate, w_up, gains)
    run_3.step(grad_mlp_gain)
    while not run_3.done():
        run_3.step()
    grad_query, grad_key, grad_value, grad_attn_gain = pl.pallas_call(
        finish_last_kernel,
        out_shape=(
            shape((rows, width), F32), shape((rows, kv), F32), shape((rows, kv), F32), gain_shape
        ),
        in_specs=[SMEM] + vmem(6),
        out_specs=vmem(4),
        compiler_params=params,
        cost_estimate=cost(3),
        name="finish_last",
    )(ids, *run_3.now, w_query, w_key, w_value, gains)
    grad_down = grad_down.T
    return (
        out.T, d_tok.T, grad_query, grad_key, grad_value, grad_out, grad_attn_gain,
        grad_gate, grad_up, grad_down, grad_mlp_gain,
    )


def solution(mesh):
    everywhere = P(("rep", "shard"), None)
    weight = P("shard", None)
    gain = P("shard")
    return jax.shard_map(
        functools.partial(shards, mesh.shape["rep"]),
        mesh=mesh,
        in_specs=(
            everywhere, everywhere, everywhere, weight, weight, weight, weight, gain, weight, weight,
            weight, gain,
        ),
        out_specs=(
            everywhere, everywhere, weight, weight, weight, weight, gain, weight, weight, weight, gain,
        ),
        check_vma=False,
    )
```

profile of v0, /device:TPU:0, one launch (start us, length us, event | category | flops | bytes accessed | tf_op | source)
XLA Modules:
  0.0 187.6 jit_solution(15053593108264179319)
XLA Ops:
  0.7 1.9 %pack_first.1.packed = bf16[160,960]{1,0:T(8,128)(2,1)} custom-call(bf16[288,576]{1,0:T(8,128)(2,1)} %wq.5, bf16[288,192]{1,0:T(8,128)(2,1)} %wk.5, bf16[288,192]{1,0:T(8,128)(2,1)} %wv.5, bf16[288]{0:T(512)(128)(2,1)} %attn_gain.1, bf16[288]{0:T(512)(128)(2,1)} %mlp_gain.1), custom_call_target="tpu_custom_call" | custom-call | flops 2000000000 | bytes 1048576 | tf_op jit(solution)/shard_map/pack_first/pallas_call | solution.py:594
  2.6 2.9 %collective-permute-start = (bf16[160,960]{1,0:T(8,128)(2,1)}, bf16[160,960]{1,0:T(8,128)(2,1)S(1)}, u32[]{:S(2)}, u32[]{:S(2)}) collective-permute-start(bf16[160,960]{1,0:T(8,128)(2,1)} %pack_first.1.packed), channel_id=1, source_target_pairs={{0,1},{1,0},{2,3},{3,2},{4,5},{5,4},{6,7},{7,6},{8,9},{9,8},{10,11... | collective-permute-start | bytes 921608 | tf_op jit(solution)/shard_map/ppermute | solution.py:581
  5.5 0.2 reduce-window.4
  5.9 0.2 select_reduce_fusion.1
  6.0 0.5 fusion.1.need
  6.5 1.3 multiply_sine_fusion
  7.8 0.6 pad_add_fusion.ids
  8.4 3.2 %pack_rest.1 = (bf16[144,3840]{1,0:T(8,128)(2,1)}, bf16[144,1536]{1,0:T(8,128)(2,1)}) custom-call(s32[2]{0:T(128)} %pad_add_fusion.ids, bf16[288,1536]{1,0:T(8,128)(2,1)} %wg.3, bf16[288,1536]{1,0:T(8,128)(2,1)} %wu.3, bf16[576,768]{1,0:T(8,128)(2,1)} %bitcast.31, bf16[288,576]{1,0:T(8,128)(2,1)} %wo_own.1), custom_call_target="tpu_custom_call" | custom-call | flops 3000000000 | bytes 1048576 | tf_op jit(solution)/shard_map/pack_rest/pallas_call | solution.py:602
  11.6 1.8 collective-permute-done.got_a
  13.5 1.7 collective-permute-start.1
  15.2 0.7 copy-done.17
  15.9 6.2 %project.1 = (bf16[576,960]{1,0:T(8,128)(2,1)}, f32[576,8]{1,0:T(8,128)}, bf16[576,1024]{1,0:T(8,128)(2,1)}, bf16[576,1024]{1,0:T(8,128)(2,1)}, bf16[192,1024]{1,0:T(8,128)(2,1)}, /*index=5*/bf16[192,1024]{1,0:T(8,128)(2,1)}) custom-call(s32[2]{0:T(128)} %pad_add_fusion.ids, bf16[576,1024]{1,0:T(8,128)(2,1)} %bitcast.28, bf16[288,576]{1,0:T(8,128)(2,1)} %wq.5, ...), custom_call_target="tpu_custom_call" | custom-call | flops 5000000000 | bytes 1048576 | tf_op jit(solution)/shard_map/project/pallas_call | solution.py:632
  22.1 5.9 %attend.3 = (f32[192,1024]{1,0:T(8,128)}, bf16[192,1024]{1,0:T(8,128)(2,1)}, f32[8,1024]{1,0:T(8,128)}) custom-call(s32[4]{0:T(128)} %fusion.1.need, s32[1,1024]{1,0:T(1,128)} %bitcast.20, bf16[576,1024]{1,0:T(8,128)(2,1)} %get-tuple-element.106.q, bf16[192,1024]{1,0:T(8,128)(2,1)} %get-tuple-element.107.k, bf16[192,1024]{1,0:T(8,128)(2,1)} %get-tuple-element.108.v), custom_call_target="tpu_custom_call" | custom-call | flops 7000000000 | bytes 1048576 | tf_op jit(solution)/shard_map/attend/pallas_call | solution.py:654
  28.0 5.4 %attend.4 = (f32[192,1024]{1,0:T(8,128)}, bf16[192,1024]{1,0:T(8,128)(2,1)}, f32[8,1024]{1,0:T(8,128)}) custom-call(s32[4]{0:T(128)} %fusion.1.need, s32[1,1024]{1,0:T(1,128)} %bitcast.21, bf16[576,1024]{1,0:T(8,128)(2,1)} %get-tuple-element.106.q, bf16[192,1024]{1,0:T(8,128)(2,1)} %get-tuple-element.107.k, bf16[192,1024]{1,0:T(8,128)(2,1)} %get-tuple-element.108.v), custom_call_target="tpu_custom_call" | custom-call | flops 7000000000 | bytes 1048576 | tf_op jit(solution)/shard_map/attend/pallas_call | solution.py:654
  33.4 5.4 %attend.5 = (f32[192,1024]{1,0:T(8,128)}, bf16[192,1024]{1,0:T(8,128)(2,1)}, f32[8,1024]{1,0:T(8,128)}) custom-call(s32[4]{0:T(128)} %fusion.1.need, s32[1,1024]{1,0:T(1,128)} %bitcast.22, bf16[576,1024]{1,0:T(8,128)(2,1)} %get-tuple-element.106.q, bf16[192,1024]{1,0:T(8,128)(2,1)} %get-tuple-element.107.k, bf16[192,1024]{1,0:T(8,128)(2,1)} %get-tuple-element.108.v), custom_call_target="tpu_custom_call" | custom-call | flops 7000000000 | bytes 1048576 | tf_op jit(solution)/shard_map/attend/pallas_call | solution.py:654
  38.8 1.7 collective-permute-done.1.wo_a.got_a
  40.5 1.8 collective-permute-start.4
  42.3 0.9 collective-permute-done.3.wo_b.got_b
  43.2 1.1 copy-done.9
  44.3 22.6 %middle_first.1 = (f32[576,1024]{1,0:T(8,128)}, bf16[576,1024]{1,0:T(8,128)(2,1)}, f32[576,1024]{1,0:T(8,128)}, f32[576,1024]{1,0:T(8,128)}, bf16[576,576]{1,0:T...) custom-call(s32[2]{0:T(128)} %pad_add_fusion.ids, ...), custom_call_target="tpu_custom_call" | custom-call | flops 17999998976 | bytes 1048576 | tf_op jit(solution)/shard_map/middle_first/pallas_call | solution.py:696
  66.9 0.2 collective-permute-start.5
  67.1 0.4 collective-permute-start.6
  67.5 2.1 %collective-permute-done.5 = bf16[144,3072]{1,0:T(8,128)(2,1)S(1)} collective-permute-done((bf16[144,3072]{1,0:T(8,128)(2,1)}, bf16[144,3072]{1,0:T(8,128)(2,1)S(1)}, u32[]{:S(2)}, u32[]{:S(2)}) %collective-permute-start.5) | collective-permute-done | bytes 884768 | tf_op jit(solution)/shard_map/ppermute | solution.py:584
  69.6 1.4 add.100
  71.0 1.8 collective-permute-start.8
  72.8 0.8 copy-done.15
  73.6 15.6 %middle_second.1 = (bf16[576,1024]{1,0:T(8,128)(2,1)}, f32[576,1024]{1,0:T(8,128)}, bf16[576,1024]{1,0:T(8,128)(2,1)}, bf16[144,2304]{1,0:T(8,128)(2,1)}, bf16[1...) custom-call(s32[2]{0:T(128)} %pad_add_fusion.ids, bf16[576,1024]{1,0:T(8,128)(2,1)} %bitcast.27, ...), custom_call_target="tpu_custom_call" | custom-call | flops 17999998976 | bytes 1048576 | tf_op jit(solution)/shard_map/middle_second/pallas_call | solution.py:766
  89.2 0.6 collective-permute-start.10
  89.8 2.1 %collective-permute-done.10 = bf16[144,2304]{1,0:T(8,128)(2,1)} collective-permute-done((bf16[144,2304]{1,0:T(8,128)(2,1)}, bf16[144,2304]{1,0:T(8,128)(2,1)}, u32[]{:S(2)}, u32[]{:S(2)}) %collective-permute-start.10) | collective-permute-done | bytes 663584 | tf_op jit(solution)/shard_map/ppermute | solution.py:584
  91.8 1.4 add.106
  93.3 0.4 collective-permute-start.13
  94.0 1.8 collective-permute-start.9
  95.8 8.5 %attend_back.3 = (bf16[320,1024]{1,0:T(8,128)(2,1)}, bf16[4,144,320]{2,1,0:T(8,128)(2,1)}) custom-call(s32[2]{0:T(128)} %pad_add_fusion.ids, s32[4]{0:T(128)} %fusion.1.need, s32[1,1024]{1,0:T(1,128)} %bitcast.23, bf16[576,1024]{1,0:T(8,128)(2,1)} %get-tuple-element.106.q, bf16[192,1024]{1,0:T(8,128)(2,1)} %get-tuple-element.107.k, ...), custom_call_target="tpu_custom_call" | custom-call | flops 10000000000 | bytes 1048576 | tf_op jit(solution)/shard_map/attend_back/pallas_call | solution.py:800
  104.2 6.3 %collective-permute-done.13 = bf16[144,2304]{1,0:T(8,128)(2,1)S(1)} collective-permute-done((bf16[144,2304]{1,0:T(8,128)(2,1)S(1)}, bf16[144,2304]{1,0:T(8,128)(2,1)S(1)}, u32[]{:S(2)}, u32[]{:S(2)}) %collective-permute-start.13) | collective-permute-done | bytes 663584 | tf_op jit(solution)/shard_map/ppermute | solution.py:581
  110.7 1.6 collective-permute-start.15
  112.4 1.6 collective-permute-start.11
  114.1 8.7 %attend_back.4 = (bf16[320,1024]{1,0:T(8,128)(2,1)}, bf16[4,144,320]{2,1,0:T(8,128)(2,1)}) custom-call(s32[2]{0:T(128)} %pad_add_fusion.ids, s32[4]{0:T(128)} %fusion.1.need, s32[1,1024]{1,0:T(1,128)} %bitcast.24, bf16[576,1024]{1,0:T(8,128)(2,1)} %get-tuple-element.106.q, bf16[192,1024]{1,0:T(8,128)(2,1)} %get-tuple-element.107.k, ...), custom_call_target="tpu_custom_call" | custom-call | flops 10000000000 | bytes 1048576 | tf_op jit(solution)/shard_map/attend_back/pallas_call | solution.py:800
  122.8 3.0 %collective-permute-start.14 = (bf16[72,1536]{1,0:T(8,128)(2,1)S(1)}, bf16[72,1536]{1,0:T(8,128)(2,1)S(1)}, u32[]{:S(2)}, u32[]{:S(2)}) collective-permute-start(bf16[72,1536]{1,0:T(8,128)(2,1)S(1)} %dynamic-slice_add_fusion.2), channel_id=1, source_target_pairs={{0,16},{2,18},{4,20},{6,22},{8,24},{10,26},{12,28},{14,30},{16,0},... | collective-permute-start | bytes 663560 | tf_op jit(solution)/shard_map/ppermute | solution.py:584
  126.0 9.3 %attend_back.5 = (bf16[320,1024]{1,0:T(8,128)(2,1)}, bf16[144,960]{1,0:T(8,128)(2,1)}, bf16[144,960]{1,0:T(8,128)(2,1)}, bf16[144,960]{1,0:T(8,128)(2,1)}, bf16[144,960]{1,0:T(8,128)(2,1)}) custom-call(s32[2]{0:T(128)} %pad_add_fusion.ids, s32[4]{0:T(128)} %fusion.1.need, s32[1,1024]{1,0:T(1,128)} %bitcast.25, bf16[576,1024]{1,0:T(8,128)(2,1)} %get-tuple-element.106.q, ...), custom_call_target="tpu_custom_call" | custom-call | flops 10000000000 | bytes 1048576 | tf_op jit(solution)/shard_map/attend_back/pallas_call | solution.py:800
  135.3 0.3 collective-permute-done.16
  135.7 1.3 collective-permute-start.25
  137.0 1.4 collective-permute-start.28
  138.5 1.1 collective-permute-start.19
  139.6 6.9 %input_grad.1 = f32[576,1024]{1,0:T(8,128)} custom-call(bf16[576,1024]{1,0:T(8,128)(2,1)} %bitcast.30, f32[576,1024]{1,0:T(8,128)} %get-tuple-element.135.d_mid, bf16[576,960]{1,0:T(8,128)(2,1)} %get-tuple-element.165.w_full, f32[576,8]{1,0:T(8,128)} %get-tuple-element.120.gains, bf16[320,1024]{1,0:T(8,128)(2,1)} %get-tuple-element.143.d0, ...), custom_call_target="tpu_custom_call" | custom-call | flops 7000000000 | bytes 1048576 | tf_op jit(solution)/shard_map/input_grad/pallas_call | solution.py:826
  146.5 0.9 collective-permute-done.19
  147.5 0.3 collective-permute-start.20
  147.9 1.3 collective-permute-start.29
  149.2 3.8 %collective-permute-done.20 = bf16[72,960]{1,0:T(8,128)(2,1)S(1)} collective-permute-done((bf16[72,960]{1,0:T(8,128)(2,1)S(1)}, bf16[72,960]{1,0:T(8,128)(2,1)S(1)}, u32[]{:S(2)}, u32[]{:S(2)}) %collective-permute-start.20) | collective-permute-done | bytes 138272 | tf_op jit(solution)/shard_map/ppermute | solution.py:584
  153.0 0.3 collective-permute-start.21
  153.5 1.1 collective-permute-start.26
  154.5 3.7 %collective-permute-done.21 = bf16[72,960]{1,0:T(8,128)(2,1)S(1)} collective-permute-done((bf16[72,960]{1,0:T(8,128)(2,1)S(1)}, bf16[72,960]{1,0:T(8,128)(2,1)S(1)}, u32[]{:S(2)}, u32[]{:S(2)}) %collective-permute-start.21) | collective-permute-done | bytes 138272 | tf_op jit(solution)/shard_map/ppermute | solution.py:584
  158.2 1.5 collective-permute-start.22
  159.9 0.8 collective-permute-start.30
  160.7 4.9 %collective-permute-done.22 = bf16[72,960]{1,0:T(8,128)(2,1)S(1)} collective-permute-done((bf16[72,960]{1,0:T(8,128)(2,1)S(1)}, bf16[72,960]{1,0:T(8,128)(2,1)S(1)}, u32[]{:S(2)}, u32[]{:S(2)}) %collective-permute-start.22) | collective-permute-done | bytes 138272 | tf_op jit(solution)/shard_map/ppermute | solution.py:584
  165.7 0.7 collective-permute-start.23
  166.4 0.2 collective-permute-done.26
  166.9 7.4 %collective-permute-done.23 = bf16[72,960]{1,0:T(8,128)(2,1)S(1)} collective-permute-done((bf16[72,960]{1,0:T(8,128)(2,1)S(1)}, bf16[72,960]{1,0:T(8,128)(2,1)S(1)}, u32[]{:S(2)}, u32[]{:S(2)}) %collective-permute-start.23) | collective-permute-done | bytes 138272 | tf_op jit(solution)/shard_map/ppermute | solution.py:584
  174.7 0.5 collective-permute-start.24
  175.1 1.6 collective-permute-done.31.got_2
  176.8 0.8 copy-done.12
  177.6 0.9 copy-done.10
  178.5 5.5 %finish_hidden.1 = (f32[288,1536]{1,0:T(8,128)}, f32[288,1536]{1,0:T(8,128)}, f32[576,768]{1,0:T(8,128)}, f32[288,576]{1,0:T(8,128)}, f32[288]{0:T(512)}) custom-call(s32[2]{0:T(128)} %pad_add_fusion.ids, bf16[144,3072]{1,0:T(8,128)(2,1)} %copy-done.1, bf16[144,3072]{1,0:T(8,128)(2,1)} %copy-done.10, bf16[144,2304]{1,0:T(8,128)(2,1)} %copy-done.2, ...), custom_call_target="tpu_custom_call" | custom-call | flops 5000000000 | bytes 1048576 | tf_op jit(solution)/shard_map/finish_hidden/pallas_call | solution.py:851
  184.0 0.7 copy-done.19
  184.7 2.6 %finish_last.1 = (f32[288,576]{1,0:T(8,128)}, f32[288,192]{1,0:T(8,128)}, f32[288,192]{1,0:T(8,128)}, f32[288]{0:T(512)}) custom-call(s32[2]{0:T(128)} %pad_add_fusion.ids, bf16[144,960]{1,0:T(8,128)(2,1)} %copy-done.5, bf16[144,960]{1,0:T(8,128)(2,1)} %copy-done.19, bf16[288,576]{1,0:T(8,128)(2,1)} %wq.5, bf16[288,192]{1,0:T(8,128)(2,1)} %wk.5, ...), custom_call_target="tpu_custom_call" | custom-call | flops 3000000000 | bytes 1048576 | tf_op jit(solution)/shard_map/finish_last/pallas_call | solution.py:866
  (92 shorter events, 2.3 us)
Async XLA Ops:
  0.6 4.9 %copy-start.20 = (s32[1,4]{1,0:T(1,128)S(1)}, s32[1,4]{1,0:T(1,128)}, u32[]{:S(2)}) copy-start(s32[1,4]{1,0:T(1,128)} %param.14) | copy-start | bytes 52
  2.6 10.9 %collective-permute-start = (bf16[160,960]{1,0:T(8,128)(2,1)}, bf16[160,960]{1,0:T(8,128)(2,1)S(1)}, u32[]{:S(2)}, u32[]{:S(2)}) collective-permute-start(bf16[160,960]{1,0:T(8,128)(2,1)} %pack_first.1.packed), channel_id=1, source_target_pairs={{0,1},{1,0},{2,3},{3,2},{4,5},{5,4},{6,7},{7,6},{8,9},{9,8},{10,11... | collective-permute-start | bytes 921608 | tf_op jit(solution)/shard_map/ppermute | solution.py:581
  5.8 5.8 %copy-start.7 = (s32[1024]{0:T(1024)}, s32[1024]{0:T(1024)S(1)}, u32[]{:S(2)}) copy-start(s32[1024]{0:T(1024)S(1)} %select_reduce_fusion) | copy-start | bytes 12292
  13.4 1.8 copy-start.16
  13.5 1.8 collective-permute-start.2
  13.5 27.0 %collective-permute-start.1 = (bf16[144,3840]{1,0:T(8,128)(2,1)}, bf16[144,3840]{1,0:T(8,128)(2,1)S(1)}, u32[]{:S(2)}, u32[]{:S(2)}) collective-permute-start(bf16[144,3840]{1,0:T(8,128)(2,1)} %get-tuple-element.104), channel_id=1, source_target_pairs={{0,1},{1,0},{2,3},{3,2},{4,5},{5,4},{6,7},{7,6},{8,9},{9,8},{10,11... | collective-permute-start | bytes 3317768 | tf_op jit(solution)/shard_map/ppermute | solution.py:581
  15.2 0.7 copy-start.17
  33.4 7.1 %copy-start.13 = (bf16[144,1536]{1,0:T(8,128)(2,1)S(1)}, bf16[144,1536]{1,0:T(8,128)(2,1)}, u32[]{:S(2)}) copy-start(bf16[144,1536]{1,0:T(8,128)(2,1)} %get-tuple-element.115) | copy-start | bytes 1327108
  40.5 2.7 %copy-start.8 = (bf16[144,3840]{1,0:T(8,128)(2,1)}, bf16[144,3840]{1,0:T(8,128)(2,1)S(1)}, u32[]{:S(2)}) copy-start(bf16[144,3840]{1,0:T(8,128)(2,1)S(1)} %collective-permute-done.1.wo_a.got_a) | copy-start | bytes 3317764
  40.5 2.7 %collective-permute-start.3 = (bf16[144,3840]{1,0:T(8,128)(2,1)S(1)}, bf16[144,3840]{1,0:T(8,128)(2,1)S(1)}, u32[]{:S(2)}, u32[]{:S(2)}) collective-permute-start(bf16[144,3840]{1,0:T(8,128)(2,1)S(1)} %collective-permute-done.1.wo_a.got_a), channel_id=1, source_target_pairs={{0,2},{2,0},{4,6},{6,4},{8,10},{10,8},{12,14},{14,12},{16,18},{18,... | collective-permute-start | bytes 3317768 | tf_op jit(solution)/shard_map/ppermute | solution.py:584
  40.5 26.4 %collective-permute-start.4 = (bf16[144,1536]{1,0:T(8,128)(2,1)S(1)}, bf16[144,1536]{1,0:T(8,128)(2,1)S(1)}, u32[]{:S(2)}, u32[]{:S(2)}) collective-permute-start(bf16[144,1536]{1,0:T(8,128)(2,1)S(1)} %copy-done.13), channel_id=1, source_target_pairs={{0,1},{1,0},{2,3},{3,2},{4,5},{5,4},{6,7},{7,6},{8,9},{9,8},{10,11... | collective-permute-start | bytes 1327112 | tf_op jit(solution)/shard_map/ppermute | solution.py:581
  43.2 1.1 copy-start.9
  66.9 4.1 %copy-start.14 = (bf16[144,1536]{1,0:T(8,128)(2,1)}, bf16[144,1536]{1,0:T(8,128)(2,1)S(1)}, u32[]{:S(2)}) copy-start(bf16[144,1536]{1,0:T(8,128)(2,1)S(1)} %collective-permute-done.4.got_a) | copy-start | bytes 1327108
  66.9 2.7 %collective-permute-start.5 = (bf16[144,3072]{1,0:T(8,128)(2,1)}, bf16[144,3072]{1,0:T(8,128)(2,1)S(1)}, u32[]{:S(2)}, u32[]{:S(2)}) collective-permute-start(bf16[144,3072]{1,0:T(8,128)(2,1)} %get-tuple-element.125), channel_id=1, source_target_pairs={{0,2},{2,0},{4,6},{6,4},{8,10},{10,8},{12,14},{14,12},{16,18},{18,... | collective-permute-start | bytes 2654216 | tf_op jit(solution)/shard_map/ppermute | solution.py:584
  67.1 5.7 %collective-permute-start.6 = (bf16[144,1536]{1,0:T(8,128)(2,1)S(1)}, bf16[144,1536]{1,0:T(8,128)(2,1)S(1)}, u32[]{:S(2)}, u32[]{:S(2)}) collective-permute-start(bf16[144,1536]{1,0:T(8,128)(2,1)S(1)} %collective-permute-done.4.got_a), channel_id=1, source_target_pairs={{0,2},{2,0},{4,6},{6,4},{8,10},{10,8},{12,14},{14,12},{16,18},{18,... | collective-permute-start | bytes 1327112 | tf_op jit(solution)/shard_map/ppermute | solution.py:584
  71.0 22.8 %collective-permute-start.8 = (bf16[144,3072]{1,0:T(8,128)(2,1)S(1)}, bf16[144,3072]{1,0:T(8,128)(2,1)S(1)}, u32[]{:S(2)}, u32[]{:S(2)}) collective-permute-start(bf16[144,3072]{1,0:T(8,128)(2,1)S(1)} %add.100), channel_id=1, source_target_pairs={{0,1},{1,0},{2,3},{3,2},{4,5},{5,4},{6,7},{7,6},{8,9},{9,8},{10,11... | collective-permute-start | bytes 2654216 | tf_op jit(solution)/shard_map/ppermute | solution.py:581
  72.8 21.0 %collective-permute-start.7 = (bf16[144,3072]{1,0:T(8,128)(2,1)}, bf16[144,3072]{1,0:T(8,128)(2,1)S(1)}, u32[]{:S(2)}, u32[]{:S(2)}) collective-permute-start(bf16[144,3072]{1,0:T(8,128)(2,1)} %get-tuple-element.134), channel_id=1, source_target_pairs={{0,2},{2,0},{4,6},{6,4},{8,10},{10,8},{12,14},{14,12},{16,18},{18,... | collective-permute-start | bytes 2654216 | tf_op jit(solution)/shard_map/ppermute | solution.py:584
  72.8 0.8 copy-start.15
  89.2 4.6 %copy-start = (bf16[144,3072]{1,0:T(8,128)(2,1)S(1)}, bf16[144,3072]{1,0:T(8,128)(2,1)}, u32[]{:S(2)}) copy-start(bf16[144,3072]{1,0:T(8,128)(2,1)} %get-tuple-element.132) | copy-start | bytes 2654212
  89.2 2.7 %collective-permute-start.10 = (bf16[144,2304]{1,0:T(8,128)(2,1)}, bf16[144,2304]{1,0:T(8,128)(2,1)}, u32[]{:S(2)}, u32[]{:S(2)}) collective-permute-start(bf16[144,2304]{1,0:T(8,128)(2,1)} %get-tuple-element.138), channel_id=1, source_target_pairs={{0,2},{2,0},{4,6},{6,4},{8,10},{10,8},{12,14},{14,12},{16,18},{18,... | collective-permute-start | bytes 1990664 | tf_op jit(solution)/shard_map/ppermute | solution.py:584
  89.8 3.9 %copy-start.11 = (bf16[144,2304]{1,0:T(8,128)(2,1)S(1)}, bf16[144,2304]{1,0:T(8,128)(2,1)}, u32[]{:S(2)}) copy-start(bf16[144,2304]{1,0:T(8,128)(2,1)} %get-tuple-element.147) | copy-start | bytes 1990660
  93.3 17.3 %collective-permute-start.13 = (bf16[144,2304]{1,0:T(8,128)(2,1)S(1)}, bf16[144,2304]{1,0:T(8,128)(2,1)S(1)}, u32[]{:S(2)}, u32[]{:S(2)}) collective-permute-start(bf16[144,2304]{1,0:T(8,128)(2,1)S(1)} %add.106), channel_id=1, source_target_pairs={{0,1},{1,0},{2,3},{3,2},{4,5},{5,4},{6,7},{7,6},{8,9},{9,8},{10,11... | collective-permute-start | bytes 1990664 | tf_op jit(solution)/shard_map/ppermute | solution.py:581
  93.7 16.9 %collective-permute-start.12 = (bf16[144,2304]{1,0:T(8,128)(2,1)S(1)}, bf16[144,2304]{1,0:T(8,128)(2,1)S(1)}, u32[]{:S(2)}, u32[]{:S(2)}) collective-permute-start(bf16[144,2304]{1,0:T(8,128)(2,1)S(1)} %copy-done.11), channel_id=1, source_target_pairs={{0,2},{2,0},{4,6},{6,4},{8,10},{10,8},{12,14},{14,12},{16,18},{18,... | collective-permute-start | bytes 1990664 | tf_op jit(solution)/shard_map/ppermute | solution.py:584
  94.0 18.3 %collective-permute-start.9 = (bf16[72,3072]{1,0:T(8,128)(2,1)S(1)}, bf16[72,3072]{1,0:T(8,128)(2,1)S(1)}, u32[]{:S(2)}, u32[]{:S(2)}) collective-permute-start(bf16[72,3072]{1,0:T(8,128)(2,1)S(1)} %constant_dynamic-slice_fusion.4), channel_id=1, source_target_pairs={{0,4},{2,6},{4,0},{6,2},{8,12},{10,14},{12,8},{14,10},{16,20},{18,... | collective-permute-start | bytes 1327112 | tf_op jit(solution)/shard_map/ppermute | solution.py:584
  95.8 14.8 %copy-start.3 = (bf16[144,2304]{1,0:T(8,128)(2,1)S(1)}, bf16[144,2304]{1,0:T(8,128)(2,1)}, u32[]{:S(2)}) copy-start(bf16[144,2304]{1,0:T(8,128)(2,1)} %get-tuple-element.145) | copy-start | bytes 1990660
  110.7 15.0 %collective-permute-start.15 = (bf16[72,2304]{1,0:T(8,128)(2,1)S(1)}, bf16[72,2304]{1,0:T(8,128)(2,1)S(1)}, u32[]{:S(2)}, u32[]{:S(2)}) collective-permute-start(bf16[72,2304]{1,0:T(8,128)(2,1)S(1)} %constant_dynamic-slice_fusion.2), channel_id=1, source_target_pairs={{0,4},{2,6},{4,0},{6,2},{8,12},{10,14},{12,8},{14,10},{16,20},{18,... | collective-permute-start | bytes 995336 | tf_op jit(solution)/shard_map/ppermute | solution.py:584
  112.4 10.3 %collective-permute-start.11 = (bf16[72,1536]{1,0:T(8,128)(2,1)S(1)}, bf16[72,1536]{1,0:T(8,128)(2,1)S(1)}, u32[]{:S(2)}, u32[]{:S(2)}) collective-permute-start(bf16[72,1536]{1,0:T(8,128)(2,1)S(1)} %constant_dynamic-slice_fusion.3), channel_id=1, source_target_pairs={{0,8},{2,10},{4,12},{6,14},{8,0},{10,2},{12,4},{14,6},{16,24},{18,... | collective-permute-start | bytes 663560 | tf_op jit(solution)/shard_map/ppermute | solution.py:584
  122.8 12.4 %collective-permute-start.14 = (bf16[72,1536]{1,0:T(8,128)(2,1)S(1)}, bf16[72,1536]{1,0:T(8,128)(2,1)S(1)}, u32[]{:S(2)}, u32[]{:S(2)}) collective-permute-start(bf16[72,1536]{1,0:T(8,128)(2,1)S(1)} %dynamic-slice_add_fusion.2), channel_id=1, source_target_pairs={{0,16},{2,18},{4,20},{6,22},{8,24},{10,26},{12,28},{14,30},{16,0},... | collective-permute-start | bytes 663560 | tf_op jit(solution)/shard_map/ppermute | solution.py:584
  125.9 9.7 %collective-permute-start.16 = (bf16[72,1152]{1,0:T(8,128)(2,1)S(1)}, bf16[72,1152]{1,0:T(8,128)(2,1)S(1)}, u32[]{:S(2)}, u32[]{:S(2)}) collective-permute-start(bf16[72,1152]{1,0:T(8,128)(2,1)S(1)} %constant_dynamic-slice_fusion.1), channel_id=1, source_target_pairs={{0,8},{2,10},{4,12},{6,14},{8,0},{10,2},{12,4},{14,6},{16,24},{18,... | collective-permute-start | bytes 497672 | tf_op jit(solution)/shard_map/ppermute | solution.py:584
  135.2 3.2 %copy-start.4 = (bf16[144,960]{1,0:T(8,128)(2,1)S(1)}, bf16[144,960]{1,0:T(8,128)(2,1)}, u32[]{:S(2)}) copy-start(bf16[144,960]{1,0:T(8,128)(2,1)} %get-tuple-element.161) | copy-start | bytes 829444
  135.2 4.4 %copy-start.18 = (bf16[144,960]{1,0:T(8,128)(2,1)S(1)}, bf16[144,960]{1,0:T(8,128)(2,1)}, u32[]{:S(2)}) copy-start(bf16[144,960]{1,0:T(8,128)(2,1)} %get-tuple-element.168) | copy-start | bytes 829444
  135.7 2.8 %collective-permute-start.17 = (bf16[144,960]{1,0:T(8,128)(2,1)}, bf16[144,960]{1,0:T(8,128)(2,1)S(1)}, u32[]{:S(2)}, u32[]{:S(2)}) collective-permute-start(bf16[144,960]{1,0:T(8,128)(2,1)} %get-tuple-element.163), channel_id=1, source_target_pairs={{0,2},{2,0},{4,6},{6,4},{8,10},{10,8},{12,14},{14,12},{16,18},{18,... | collective-permute-start | bytes 829448 | tf_op jit(solution)/shard_map/ppermute | solution.py:584
  135.7 13.5 %collective-permute-start.25 = (bf16[72,1536]{1,0:T(8,128)(2,1)S(1)}, bf16[72,1536]{1,0:T(8,128)(2,1)S(1)}, u32[]{:S(2)}, u32[]{:S(2)}) collective-permute-start(bf16[72,1536]{1,0:T(8,128)(2,1)S(1)} %add.116), channel_id=1, source_target_pairs={{0,8},{2,10},{4,12},{6,14},{8,0},{10,2},{12,4},{14,6},{16,24},{18,... | collective-permute-start | bytes 663560 | tf_op jit(solution)/shard_map/ppermute | solution.py:584
  137.0 10.8 %collective-permute-start.28 = (bf16[72,1152]{1,0:T(8,128)(2,1)S(1)}, bf16[72,1152]{1,0:T(8,128)(2,1)S(1)}, u32[]{:S(2)}, u32[]{:S(2)}) collective-permute-start(bf16[72,1152]{1,0:T(8,128)(2,1)S(1)} %dynamic-slice_add_fusion.3), channel_id=1, source_target_pairs={{0,16},{2,18},{4,20},{6,22},{8,24},{10,26},{12,28},{14,30},{16,0},... | collective-permute-start | bytes 497672 | tf_op jit(solution)/shard_map/ppermute | solution.py:584
  138.5 8.9 %collective-permute-start.19 = (bf16[144,960]{1,0:T(8,128)(2,1)S(1)}, bf16[144,960]{1,0:T(8,128)(2,1)S(1)}, u32[]{:S(2)}, u32[]{:S(2)}) collective-permute-start(bf16[144,960]{1,0:T(8,128)(2,1)S(1)} %add.119), channel_id=1, source_target_pairs={{0,1},{1,0},{2,3},{3,2},{4,5},{5,4},{6,7},{7,6},{8,9},{9,8},{10,11... | collective-permute-start | bytes 829448 | tf_op jit(solution)/shard_map/ppermute | solution.py:581
  139.6 7.8 %collective-permute-start.18 = (bf16[144,960]{1,0:T(8,128)(2,1)S(1)}, bf16[144,960]{1,0:T(8,128)(2,1)S(1)}, u32[]{:S(2)}, u32[]{:S(2)}) collective-permute-start(bf16[144,960]{1,0:T(8,128)(2,1)S(1)} %copy-done.18), channel_id=1, source_target_pairs={{0,2},{2,0},{4,6},{6,4},{8,10},{10,8},{12,14},{14,12},{16,18},{18,... | collective-permute-start | bytes 829448 | tf_op jit(solution)/shard_map/ppermute | solution.py:584
  139.6 7.8 %copy-start.6 = (bf16[144,960]{1,0:T(8,128)(2,1)S(1)}, bf16[144,960]{1,0:T(8,128)(2,1)}, u32[]{:S(2)}) copy-start(bf16[144,960]{1,0:T(8,128)(2,1)} %get-tuple-element.166) | copy-start | bytes 829444
  147.5 5.5 %collective-permute-start.20 = (bf16[72,960]{1,0:T(8,128)(2,1)S(1)}, bf16[72,960]{1,0:T(8,128)(2,1)S(1)}, u32[]{:S(2)}, u32[]{:S(2)}) collective-permute-start(bf16[72,960]{1,0:T(8,128)(2,1)S(1)} %constant_dynamic-slice_fusion), channel_id=1, source_target_pairs={{0,4},{2,6},{4,0},{6,2},{8,12},{10,14},{12,8},{14,10},{16,20},{18,... | collective-permute-start | bytes 414728 | tf_op jit(solution)/shard_map/ppermute | solution.py:584
  147.9 6.7 %collective-permute-start.29 = (bf16[72,1152]{1,0:T(8,128)(2,1)S(1)}, bf16[72,1152]{1,0:T(8,128)(2,1)S(1)}, u32[]{:S(2)}, u32[]{:S(2)}) collective-permute-start(bf16[72,1152]{1,0:T(8,128)(2,1)S(1)} %add.125), channel_id=1, source_target_pairs={{0,8},{2,10},{4,12},{6,14},{8,0},{10,2},{12,4},{14,6},{16,24},{18,... | collective-permute-start | bytes 497672 | tf_op jit(solution)/shard_map/ppermute | solution.py:584
  153.0 5.2 %collective-permute-start.21 = (bf16[72,960]{1,0:T(8,128)(2,1)S(1)}, bf16[72,960]{1,0:T(8,128)(2,1)S(1)}, u32[]{:S(2)}, u32[]{:S(2)}) collective-permute-start(bf16[72,960]{1,0:T(8,128)(2,1)S(1)} %dynamic-slice_add_fusion.4), channel_id=1, source_target_pairs={{0,8},{2,10},{4,12},{6,14},{8,0},{10,2},{12,4},{14,6},{16,24},{18,... | collective-permute-start | bytes 414728 | tf_op jit(solution)/shard_map/ppermute | solution.py:584
  153.5 13.2 %collective-permute-start.26 = (bf16[72,3072]{1,0:T(8,128)(2,1)S(1)}, bf16[72,3072]{1,0:T(8,128)(2,1)S(1)}, u32[]{:S(2)}, u32[]{:S(2)}) collective-permute-start(bf16[72,3072]{1,0:T(8,128)(2,1)S(1)} %maximum_select_fusion.2), channel_id=1, source_target_pairs={{0,4},{2,6},{4,0},{6,2},{8,12},{10,14},{12,8},{14,10},{16,20},{18,... | collective-permute-start | bytes 1327112 | tf_op jit(solution)/shard_map/ppermute | solution.py:584
  158.2 7.4 %collective-permute-start.22 = (bf16[72,960]{1,0:T(8,128)(2,1)S(1)}, bf16[72,960]{1,0:T(8,128)(2,1)S(1)}, u32[]{:S(2)}, u32[]{:S(2)}) collective-permute-start(bf16[72,960]{1,0:T(8,128)(2,1)S(1)} %add.123), channel_id=1, source_target_pairs={{0,16},{2,18},{4,20},{6,22},{8,24},{10,26},{12,28},{14,30},{16,0},... | collective-permute-start | bytes 414728 | tf_op jit(solution)/shard_map/ppermute | solution.py:584
  159.9 14.5 %collective-permute-start.30 = (bf16[72,2304]{1,0:T(8,128)(2,1)S(1)}, bf16[72,2304]{1,0:T(8,128)(2,1)S(1)}, u32[]{:S(2)}, u32[]{:S(2)}) collective-permute-start(bf16[72,2304]{1,0:T(8,128)(2,1)S(1)} %maximum_select_fusion.3), channel_id=1, source_target_pairs={{0,4},{2,6},{4,0},{6,2},{8,12},{10,14},{12,8},{14,10},{16,20},{18,... | collective-permute-start | bytes 995336 | tf_op jit(solution)/shard_map/ppermute | solution.py:584
  165.7 8.7 %collective-permute-start.23 = (bf16[72,960]{1,0:T(8,128)(2,1)S(1)}, bf16[72,960]{1,0:T(8,128)(2,1)S(1)}, u32[]{:S(2)}, u32[]{:S(2)}) collective-permute-start(bf16[72,960]{1,0:T(8,128)(2,1)S(1)} %add.124), channel_id=1, source_target_pairs={{0,4},{2,6},{4,0},{6,2},{8,12},{10,14},{12,8},{14,10},{16,20},{18,... | collective-permute-start | bytes 414728 | tf_op jit(solution)/shard_map/ppermute | solution.py:584
  166.8 9.9 %copy-start.1 = (bf16[144,3072]{1,0:T(8,128)(2,1)}, bf16[144,3072]{1,0:T(8,128)(2,1)S(1)}, u32[]{:S(2)}) copy-start(bf16[144,3072]{1,0:T(8,128)(2,1)S(1)} %maximum_select_fusion.mine_1) | copy-start | bytes 2654212
  166.8 9.9 %collective-permute-start.27 = (bf16[144,3072]{1,0:T(8,128)(2,1)S(1)}, bf16[144,3072]{1,0:T(8,128)(2,1)S(1)}, u32[]{:S(2)}, u32[]{:S(2)}) collective-permute-start(bf16[144,3072]{1,0:T(8,128)(2,1)S(1)} %maximum_select_fusion.mine_1), channel_id=1, source_target_pairs={{0,2},{2,0},{4,6},{6,4},{8,10},{10,8},{12,14},{14,12},{16,18},{18,... | collective-permute-start | bytes 2654216 | tf_op jit(solution)/shard_map/ppermute | solution.py:584
  174.4 9.6 %copy-start.5 = (bf16[144,960]{1,0:T(8,128)(2,1)}, bf16[144,960]{1,0:T(8,128)(2,1)S(1)}, u32[]{:S(2)}) copy-start(bf16[144,960]{1,0:T(8,128)(2,1)S(1)} %maximum_select_fusion.4.mine) | copy-start | bytes 829444
  174.6 2.2 %copy-start.2 = (bf16[144,2304]{1,0:T(8,128)(2,1)}, bf16[144,2304]{1,0:T(8,128)(2,1)S(1)}, u32[]{:S(2)}) copy-start(bf16[144,2304]{1,0:T(8,128)(2,1)S(1)} %maximum_select_fusion.1.mine_2) | copy-start | bytes 1990660
  174.6 2.2 %collective-permute-start.31 = (bf16[144,2304]{1,0:T(8,128)(2,1)S(1)}, bf16[144,2304]{1,0:T(8,128)(2,1)S(1)}, u32[]{:S(2)}, u32[]{:S(2)}) collective-permute-start(bf16[144,2304]{1,0:T(8,128)(2,1)S(1)} %maximum_select_fusion.1.mine_2), channel_id=1, source_target_pairs={{0,2},{2,0},{4,6},{6,4},{8,10},{10,8},{12,14},{14,12},{16,18},{18,... | collective-permute-start | bytes 1990664 | tf_op jit(solution)/shard_map/ppermute | solution.py:584
  174.7 9.4 %collective-permute-start.24 = (bf16[144,960]{1,0:T(8,128)(2,1)S(1)}, bf16[144,960]{1,0:T(8,128)(2,1)S(1)}, u32[]{:S(2)}, u32[]{:S(2)}) collective-permute-start(bf16[144,960]{1,0:T(8,128)(2,1)S(1)} %maximum_select_fusion.4.mine), channel_id=1, source_target_pairs={{0,2},{2,0},{4,6},{6,4},{8,10},{10,8},{12,14},{14,12},{16,18},{18,... | collective-permute-start | bytes 829448 | tf_op jit(solution)/shard_map/ppermute | solution.py:584
  176.7 0.8 copy-start.12
  177.6 0.9 copy-start.10
  184.0 0.7 copy-start.19
where the time goes:
time: 191 us; the launch traced here: 188 us
  Pallas kernels  108 us (57%)
  waiting for transfers between devices  37.8 us (20%)
  starting transfers between devices  28.6 us (15%)
  other arithmetic  7.17 us (4%)
  local copies, waits for them, and re-layouts  5.22 us (3%)
    ppermute x26, waiting for transfers between devices, over_rep(): return lax.ppermute(value, 'rep', [(i, i ^ 1 << bit) for i in range(size)])  27.1 us
    pallas_call x3, Pallas kernels, shards(): pl.pallas_call(attend_back_kernel, grid=(1,), out_shape=(shape((GD, count...  26.4 us
    pallas_call x1, Pallas kernels, shards(): pl.pallas_call(middle_first_kernel, grid=(steps[0],), out_shape=(shape((w...  22.6 us
    ppermute x26, starting transfers between devices, over_rep(): return lax.ppermute(value, 'rep', [(i, i ^ 1 << bit) for i in range(size)])  18.9 us
    pallas_call x3, Pallas kernels, shards(): pl.pallas_call(attend_kernel, grid=(1,), out_shape=(shape((GQ, count), F3...  16.7 us
    pallas_call x1, Pallas kernels, shards(): pl.pallas_call(middle_second_kernel, grid=(steps[1],), out_shape=(shape((...  15.6 us
    ppermute x6, waiting for transfers between devices, over_x(): return lax.ppermute(value, 'shard', [(0, 1), (1, 0)])  10.7 us
    ppermute x6, starting transfers between devices, over_x(): return lax.ppermute(value, 'shard', [(0, 1), (1, 0)])  9.76 us
  transfers between devices with their start and end apart: 32, of which 14 were waited for; matrix products, arithmetic and copies ran while one was open for 4% of the time, Pallas kernels for 55%

commit v1 on v0

--- a/solution.py
+++ b/solution.py
@@ -243,7 +243,7 @@
 
 
 def middle_first_kernel(
-    ids, tok, cot, att0, att1, att2, gains, wo_own, wo_a, wo_b,
+    ids, tok, cot, att, gains, wo_own, wo_a, wo_b,
     wg_lo, wg_hi, wu_lo, wu_hi, wd_own, got_a, got_b,
     mid_out, nm_out, acc_out, acc_e, wo_out, grads_0, grads_1, grads_2, grads_3,
     wg, wu, wd, nm_rows, cot_rows, mid, nm, wo, grads, sems, grad_sems,
@@ -267,8 +267,7 @@
         put_rows(wo, wo_own, wo_a.at[:, :width], wo_b.at[:, :width], ids[0], ids[1])
         copies[2].start()
         gain = gains[:, 1:2]
-        att = jnp.concatenate([att0[...], att1[...], att2[...]], axis=0)
-        mid[...] = tok[...].astype(F32) + dot_tn(wo[...], att)
+        mid[...] = tok[...].astype(F32) + dot_tn(wo[...], att[...])
         copies[0].start()
         for at in range(0, tok.shape[1], BLOCK):
             lanes = slice(at, at + BLOCK)
@@ -299,21 +298,19 @@
 
 
 def middle_second_kernel(
-    ids, cot, nm, gains, att0, att1, att2, wo_in, mid_in, out_in, e_in,
+    ids, cot, nm, gains, att_in, wo_in, mid_in, out_in, e_in,
     wg_lo, wg_hi, wu_lo, wu_hi, wd_own, got_a, got_b,
     out_out, d_mid_out, d_att_out, grads_0, grads_1, grads_2, grads_3,
     wg, wu, wd, nm_rows, cot_rows, acc_out, acc_e, att, wo, mid, out_first, e_first, out, d_att, grads,
     sems, grad_sems,
 ):
     step = pl.program_id(0)
-    rows = att0.shape[0]
     arrive = [
-        (att0, att.at[:rows, :]), (att1, att.at[rows : 2 * rows, :]), (att2, att.at[2 * rows :, :]),
-        (wo_in, wo), (mid_in, mid), (out_in, out_first), (e_in, e_first),
+        (att_in, att), (wo_in, wo), (mid_in, mid), (out_in, out_first), (e_in, e_first),
     ]
     arrive = [pltpu.make_async_copy(*pair, sems.at[at]) for at, pair in enumerate(arrive)]
     leave = [(out, out_out), (mid, d_mid_out), (d_att, d_att_out)]
-    leave = [pltpu.make_async_copy(*pair, sems.at[7 + at]) for at, pair in enumerate(leave)]
+    leave = [pltpu.make_async_copy(*pair, sems.at[len(arrive) + at]) for at, pair in enumerate(leave)]
     grads_leave = [
         pltpu.make_async_copy(grads.at[at], out_at, grad_sems.at[at])
         for at, out_at in enumerate((grads_0, grads_1, grads_2, grads_3))
@@ -372,8 +369,8 @@
 
 def attend_back_kernel(ids, need, starts, q, k, v, d_att, att, lse, cos, sin, normed, *refs):
     *refs, dk_acc, dv_acc, k_rows, v_rows = refs
-    earlier = refs[:2] if len(refs) > 2 else []
-    d_out, *targets = refs[len(earlier) :]
+    *earlier, d_out = refs[: len(refs) - (4 if len(refs) > 2 else 1)]
+    targets = refs[len(earlier) + 1 :]
     count = q.shape[1]
     half = HD // 2
     k_rows[...] = k[...].T
@@ -434,10 +431,10 @@
             target[:, at * GD : (at + 1) * GD] = group[away]
 
 
-def input_kernel(tok, d_mid, w_full, gains, d0, d1, d2, d_tok, d_all):
+def input_kernel(tok, d_mid, w_full, gains, d_0, d_1, d_2, d_tok, d_all):
     width, count = tok.shape
     kv = KVH * HD
-    for g, part in enumerate((d0, d1, d2)):
+    for g, part in enumerate((d_0, d_1, d_2)):
         d_all[g * GQ : (g + 1) * GQ, :] = part[:GQ, :]
         d_all[width + g * HD : width + (g + 1) * HD, :] = part[GQ : GQ + HD, :]
         d_all[width + kv + g * HD : width + kv + (g + 1) * HD, :] = part[GQ + HD :, :]
@@ -591,6 +588,7 @@
     cot = cotangent.T
     down = w_down.T
     params = pltpu.CompilerParams(vmem_limit_bytes=56 * MIB)
+    most = pltpu.CompilerParams(vmem_limit_bytes=62 * MIB)
     packed = pl.pallas_call(
         pack_first_kernel,
         out_shape=shape((quarter + 16, width + 2 * kv), BF16),
@@ -627,7 +625,6 @@
 
     first_a = after(over_x(packed), second, cos, sin, starts, need)
     first_b = over_rep(first_a, 0)
-    second = after(second, first_a)
 
     w_full, gains, normed, q, k, v = pl.pallas_call(
         project_kernel,
@@ -641,32 +638,32 @@
         ),
         in_specs=[SMEM] + vmem(9),
         out_specs=vmem(6),
-        compiler_params=params,
+        compiler_params=most,
         cost_estimate=cost(5),
         name="project",
     )(after(ids, second), tok, w_query, w_key, w_value, packed, first_a, first_b, cos, sin)
 
-    def one(size_of, index):
-        return pl.BlockSpec((size_of, count), lambda i: (index, 0))
-
-    atts, lows, lses = [], [], []
-    for g in range(KVH):
-        att, low, lse = pl.pallas_call(
-            attend_kernel,
-            grid=(1,),
-            out_shape=(shape((GQ, count), F32), shape((GQ, count), BF16), shape((8, count), F32)),
-            in_specs=[SMEM, one(1, 0), one(GQ, g), one(HD, g), one(HD, g)],
-            out_specs=(one(GQ, 0), one(GQ, 0), one(8, 0)),
-            scratch_shapes=[pltpu.VMEM((count, HD), BF16)],
-            compiler_params=params,
-            cost_estimate=cost(7),
-            name="attend",
-        )(after(need, *lses[-1:]), starts, q, k, v)
-        atts.append(att)
-        lows.append(low)
-        lses.append(lse)
-
-    second_a = after(over_x(second), lses[-1])
+    def grouped(size_of, first=0):
+        return pl.BlockSpec((size_of, count), lambda i: (first + i, 0))
+
+    def shared(size_of):
+        return pl.BlockSpec((size_of, count), lambda i: (0, 0))
+
+    att, low, lse = pl.pallas_call(
+        attend_kernel,
+        grid=(KVH,),
+        out_shape=(
+            shape((width, count), F32), shape((width, count), BF16), shape((8 * KVH, count), F32)
+        ),
+        in_specs=[SMEM, shared(1), grouped(GQ), grouped(HD), grouped(HD)],
+        out_specs=(grouped(GQ), grouped(GQ), grouped(8)),
+        scratch_shapes=[pltpu.VMEM((count, HD), BF16)],
+        compiler_params=params,
+        cost_estimate=cost(17),
+        name="attend",
+    )(need, starts, q, k, v)
+
+    second_a = after(over_x(second), lse)
     third = after(third, second_a)
     second_b = over_rep(second_a, 0)
 
@@ -686,10 +683,9 @@
 
     wide = whole((width, count))
     anywhere = pl.BlockSpec(memory_space=pl.ANY)
-    att_specs = [whole((GQ, count))] * KVH
     grad_shapes = [
         shape((quarter, chunk * steps[0]), BF16),
-        shape((quarter, chunk * (steps[1] + 1)), BF16),
+        shape((quarter, chunk * steps[1] + width), BF16),
     ]
     weight_scratch = [pltpu.VMEM((width, 2 * lane), BF16)] * 3 + [pltpu.VMEM((count, width), BF16)] * 2
     wo_spec = pl.BlockSpec((quarter, chunk), lambda i: (0, steps[0]))
@@ -704,7 +700,7 @@
             shape((width, width), BF16),
             *[grad_shapes[0]] * 4,
         ),
-        in_specs=[SMEM, wide, wide] + att_specs
+        in_specs=[SMEM, wide, wide, wide]
         + [whole((width, 8)), whole((rows, width)), wo_spec, wo_spec] + hidden_specs(0),
         out_specs=(anywhere, anywhere, wide, wide, anywhere) + (anywhere,) * 4,
         scratch_shapes=weight_scratch
@@ -716,11 +712,11 @@
             pltpu.SemaphoreType.DMA((3,)),
             pltpu.SemaphoreType.DMA((4,)),
         ],
-        compiler_params=params,
+        compiler_params=most,
         cost_estimate=cost(18),
         name="middle_first",
     )(
-        after(ids, third), tok, cot, *lows, gains, w_out, second_a, second_b,
+        after(ids, third), tok, cot, low, gains, w_out, second_a, second_b,
         w_gate, w_gate, w_up, w_up, down, second_a, second_b,
     )
 
@@ -772,7 +768,7 @@
             shape((width, count), BF16),
             *[grad_shapes[1]] * 4,
         ),
-        in_specs=[SMEM, wide, wide, whole((width, 8))] + [anywhere] * (KVH + 4) + hidden_specs(1),
+        in_specs=[SMEM, wide, wide, whole((width, 8))] + [anywhere] * 5 + hidden_specs(1),
         out_specs=(
             *[anywhere] * 7,
         ),
@@ -782,44 +778,42 @@
         + [pltpu.VMEM((width, count), F32)] * 3
         + [pltpu.VMEM((width, count), BF16)] * 2
         + [pltpu.VMEM((4, *grad_shapes[1].shape), BF16)]
-        + [pltpu.SemaphoreType.DMA((10,)), pltpu.SemaphoreType.DMA((4,))],
-        compiler_params=params,
+        + [pltpu.SemaphoreType.DMA((8,)), pltpu.SemaphoreType.DMA((4,))],
+        compiler_params=most,
         cost_estimate=cost(18),
         name="middle_second",
     )(
-        after(ids, run_1.step()), cot, nm, gains, *lows, wo, mid, acc_out, acc_e,
+        after(ids, run_1.step()), cot, nm, gains, low, wo, mid, acc_out, acc_e,
         w_gate, w_gate, w_up, w_up, down, third_a, third_b,
     )
     run_2 = Stages(reduce_steps(*grads_2, {1: 0, 2: 1}))
     sent = [run_1.step(d_mid), run_2.step()]
 
-    d_parts, earlier = [], []
-    for g in range(KVH):
-        joined = earlier if g == KVH - 1 else []
-        grads_to = [(quarter, GD * KVH)] * 4 if joined else [(4, quarter, GD)]
-        d_part, *pair = pl.pallas_call(
+    def attend_back(group, sent, joined, grad_dims):
+        return pl.pallas_call(
             attend_back_kernel,
             grid=(1,),
-            out_shape=(
-                shape((GD, count), BF16),
-                *[shape(dims, BF16) for dims in grads_to],
-            ),
+            out_shape=(shape((GD, count), BF16), *[shape(dims, BF16) for dims in grad_dims]),
             in_specs=[
-                SMEM, SMEM, one(1, 0), one(GQ, g), one(HD, g), one(HD, g), one(GQ, g), one(GQ, 0),
-                one(8, 0), one(HD // 2, 0), one(HD // 2, 0), one(width, 0),
+                SMEM, SMEM, shared(1), grouped(GQ, group), grouped(HD, group), grouped(HD, group),
+                grouped(GQ, group), grouped(GQ, group), grouped(8, group), shared(HD // 2),
+                shared(HD // 2), shared(width),
             ] + [whole(x.shape) for x in joined],
-            out_specs=(one(GD, 0), *[whole(dims) for dims in grads_to]),
+            out_specs=(grouped(GD), *[whole(dims) for dims in grad_dims]),
             scratch_shapes=[pltpu.VMEM((HD, count), F32)] * 2 + [pltpu.VMEM((count, HD), BF16)] * 2,
             compiler_params=params,
-            cost_estimate=cost(10),
+            cost_estimate=cost(9),
             name="attend_back",
         )(
-            after(ids, *sent), need, starts, q, k, v, d_att, atts[g], lses[g],
-            cos, sin, normed, *joined,
+            after(ids, *sent), need, starts, q, k, v, d_att, att, lse, cos, sin, normed, *joined,
         )
-        d_parts.append(d_part)
-        earlier += pair
-        sent = [run_1.step(d_part), run_2.step(d_part)]
+
+    d_0, grads_a = attend_back(0, sent, [], [(4, quarter, GD)])
+    sent = [run_1.step(d_0), run_2.step(d_0)]
+    d_1, grads_b = attend_back(1, sent, [], [(4, quarter, GD)])
+    sent = [run_1.step(d_1), run_2.step(d_1)]
+    d_2, *pair = attend_back(2, sent, [grads_a, grads_b], [(quarter, KVH * GD)] * 4)
+    sent = [run_1.step(d_2), run_2.step(d_2)]
     run_3 = Stages(reduce_steps(*pair[:3], after(pair[3], *sent), {1: 0}))
     sent.append(run_3.step())
 
@@ -832,7 +826,7 @@
         compiler_params=params,
         cost_estimate=cost(7),
         name="input_grad",
-    )(after(tok, *sent), d_mid, w_full, gains, *d_parts)
+    )(after(tok, *sent), d_mid, w_full, gains, d_0, d_1, d_2)
 
     sent = run_3.step(d_tok)
     run_1.step(after(d_tok, sent))
@@ -856,7 +850,7 @@
         ),
         in_specs=[SMEM] + vmem(7),
         out_specs=vmem(5),
-        compiler_params=params,
+        compiler_params=most,
         cost_estimate=cost(5),
         name="finish_hidden",
     )(after(ids, sent), *run_1.now, *run_2.now, w_gate, w_up, gains)
@@ -870,7 +864,7 @@
         ),
         in_specs=[SMEM] + vmem(6),
         out_specs=vmem(4),
-        compiler_params=params,
+        compiler_params=most,
         cost_estimate=cost(3),
         name="finish_last",
     )(ids, *run_3.now, w_query, w_key, w_value, gains)

time: 191 us -> 189 us (0.990)
  waiting for transfers between devices: 37.8 us -> 46.9 us
  Pallas kernels: 108 us -> 101 us
  starting transfers between devices: 28.6 us -> 25.9 us
  local copies, waits for them, and re-layouts: 5.22 us -> 2.83 us
    pallas_call x6 -> x4, Pallas kernels: 43 us -> 36.2 us  [the longest x3 25 us: attend_back(): pl.pallas_call(attend_back_kernel, grid=(1,), out_shape=(shape((GD, count...]
    ppermute x6, waiting for transfers between devices: 10.7 us -> 16.8 us  [over_x(): return lax.ppermute(value, 'shard', [(0, 1), (1, 0)])]
    ppermute x26, waiting for transfers between devices: 27.1 us -> 30.1 us  [over_rep(): return lax.ppermute(value, 'rep', [(i, i ^ 1 << bit) for i in range(size)])]
    unnamed x42 -> x34, local copies, waits for them, and re-layouts: 5.08 us -> 2.59 us
  transfers between devices with their start and end apart: 32 -> 32, of which waited for: 14 -> 15; matrix products, arithmetic and copies ran while one was open for 4% -> 4% of each run, Pallas kernels for 55% -> 52%
where the time goes in v1:
time: 189 us; the launch traced here: 186 us
  Pallas kernels  101 us (53%)
  waiting for transfers between devices  46.9 us (25%)
  starting transfers between devices  25.9 us (14%)
  other arithmetic  8.09 us (4%)
  local copies, waits for them, and re-layouts  2.83 us (1%)
    ppermute x26, waiting for transfers between devices, over_rep(): return lax.ppermute(value, 'rep', [(i, i ^ 1 << bit) for i in range(size)])  30.1 us
    pallas_call x3, Pallas kernels, attend_back(): pl.pallas_call(attend_back_kernel, grid=(1,), out_shape=(shape((GD, count...  25 us
    pallas_call x1, Pallas kernels, shards(): pl.pallas_call(middle_first_kernel, grid=(steps[0],), out_shape=(shape((w...  22.4 us
    ppermute x26, starting transfers between devices, over_rep(): return lax.ppermute(value, 'rep', [(i, i ^ 1 << bit) for i in range(size)])  17.3 us
    ppermute x6, waiting for transfers between devices, over_x(): return lax.ppermute(value, 'shard', [(0, 1), (1, 0)])  16.8 us
    pallas_call x1, Pallas kernels, shards(): pl.pallas_call(middle_second_kernel, grid=(steps[1],), out_shape=(shape((...  15.8 us
    pallas_call x1, Pallas kernels, shards(): pl.pallas_call(attend_kernel, grid=(KVH,), out_shape=(shape((width, count...  11.1 us
    ppermute x6, starting transfers between devices, over_x(): return lax.ppermute(value, 'shard', [(0, 1), (1, 0)])  8.66 us
  transfers between devices with their start and end apart: 32, of which 15 were waited for; matrix products, arithmetic and copies ran while one was open for 4% of the time, Pallas kernels for 52%

profile of v1, /device:TPU:0, one launch (start us, length us, event | category | flops | bytes accessed | tf_op | source)
XLA Modules:
  0.0 185.6 jit_solution(11299379846319249585)
XLA Ops:
  0.7 1.9 %pack_first.1.packed = bf16[160,960]{1,0:T(8,128)(2,1)} custom-call(bf16[288,576]{1,0:T(8,128)(2,1)} %wq.5, bf16[288,192]{1,0:T(8,128)(2,1)} %wk.5, bf16[288,192]{1,0:T(8,128)(2,1)} %wv.5, bf16[288]{0:T(512)(128)(2,1)} %attn_gain.1, bf16[288]{0:T(512)(128)(2,1)} %mlp_gain.1), custom_call_target="tpu_custom_call" | custom-call | flops 2000000000 | bytes 1048576 | tf_op jit(solution)/shard_map/pack_first/pallas_call | solution.py:592
  2.6 2.9 %collective-permute-start.1 = (bf16[160,960]{1,0:T(8,128)(2,1)}, bf16[160,960]{1,0:T(8,128)(2,1)S(1)}, u32[]{:S(2)}, u32[]{:S(2)}) collective-permute-start(bf16[160,960]{1,0:T(8,128)(2,1)} %pack_first.1.packed), channel_id=1, source_target_pairs={{0,1},{1,0},{2,3},{3,2},{4,5},{5,4},{6,7},{7,6},{8,9},{9,8},{10,11... | collective-permute-start | bytes 921608 | tf_op jit(solution)/shard_map/ppermute | solution.py:578
  5.5 0.2 reduce-window.4
  5.9 0.2 select_reduce_fusion.1
  6.0 0.5 fusion.1.need
  6.6 1.2 multiply_sine_fusion
  7.8 0.6 pad_add_fusion.ids
  8.4 3.2 %pack_rest.1 = (bf16[144,3840]{1,0:T(8,128)(2,1)}, bf16[144,1536]{1,0:T(8,128)(2,1)}) custom-call(s32[2]{0:T(128)} %pad_add_fusion.ids, bf16[288,1536]{1,0:T(8,128)(2,1)} %wg.3, bf16[288,1536]{1,0:T(8,128)(2,1)} %wu.3, bf16[576,768]{1,0:T(8,128)(2,1)} %bitcast.29, bf16[288,576]{1,0:T(8,128)(2,1)} %wo_own.1), custom_call_target="tpu_custom_call" | custom-call | flops 3000000000 | bytes 1048576 | tf_op jit(solution)/shard_map/pack_rest/pallas_call | solution.py:600
  11.6 1.8 collective-permute-done.1.got_a
  13.5 1.7 collective-permute-start
  15.2 0.7 copy-done.14
  15.9 6.2 %project.1 = (bf16[576,960]{1,0:T(8,128)(2,1)}, f32[576,8]{1,0:T(8,128)}, bf16[576,1024]{1,0:T(8,128)(2,1)}, bf16[576,1024]{1,0:T(8,128)(2,1)}, bf16[192,1024]{1,0:T(8,128)(2,1)}, /*index=5*/bf16[192,1024]{1,0:T(8,128)(2,1)}) custom-call(s32[2]{0:T(128)} %pad_add_fusion.ids, bf16[576,1024]{1,0:T(8,128)(2,1)} %bitcast.26, bf16[288,576]{1,0:T(8,128)(2,1)} %wq.5, ...), custom_call_target="tpu_custom_call" | custom-call | flops 5000000000 | bytes 1048576 | tf_op jit(solution)/shard_map/project/pallas_call | solution.py:629
  22.1 11.1 %attend.1 = (f32[576,1024]{1,0:T(8,128)}, bf16[576,1024]{1,0:T(8,128)(2,1)}, f32[24,1024]{1,0:T(8,128)}) custom-call(s32[4]{0:T(128)} %fusion.1.need, s32[1,1024]{1,0:T(1,128)} %bitcast.20, bf16[576,1024]{1,0:T(8,128)(2,1)} %get-tuple-element.96.q, bf16[192,1024]{1,0:T(8,128)(2,1)} %get-tuple-element.97.k, bf16[192,1024]{1,0:T(8,128)(2,1)} %get-tuple-element.98.v), custom_call_target="tpu_custom_call" | custom-call | flops 16999999488 | bytes 1048576 | tf_op jit(solution)/shard_map/attend/pallas_call | solution.py:652
  33.2 7.2 %collective-permute-done.wo_a.got_a = bf16[144,3840]{1,0:T(8,128)(2,1)S(1)} collective-permute-done((bf16[144,3840]{1,0:T(8,128)(2,1)}, bf16[144,3840]{1,0:T(8,128)(2,1)S(1)}, u32[]{:S(2)}, u32[]{:S(2)}) %collective-permute-start) | collective-permute-done | bytes 1105952 | tf_op jit(solution)/shard_map/ppermute | solution.py:578
  40.5 1.8 collective-permute-start.4
  42.3 0.9 collective-permute-done.3.wo_b.got_b
  43.2 1.0 copy-done.9
  44.2 22.4 %middle_first.1 = (f32[576,1024]{1,0:T(8,128)}, bf16[576,1024]{1,0:T(8,128)(2,1)}, f32[576,1024]{1,0:T(8,128)}, f32[576,1024]{1,0:T(8,128)}, bf16[576,576]{1,0:T...) custom-call(s32[2]{0:T(128)} %pad_add_fusion.ids, ...), custom_call_target="tpu_custom_call" | custom-call | flops 17999998976 | bytes 1048576 | tf_op jit(solution)/shard_map/middle_first/pallas_call | solution.py:692
  66.6 0.2 collective-permute-start.5
  66.8 0.4 collective-permute-start.6
  67.2 2.1 %collective-permute-done.5 = bf16[144,3072]{1,0:T(8,128)(2,1)S(1)} collective-permute-done((bf16[144,3072]{1,0:T(8,128)(2,1)}, bf16[144,3072]{1,0:T(8,128)(2,1)S(1)}, u32[]{:S(2)}, u32[]{:S(2)}) %collective-permute-start.5) | collective-permute-done | bytes 884768 | tf_op jit(solution)/shard_map/ppermute | solution.py:581
  69.3 2.4 %add.100 = bf16[144,3072]{1,0:T(8,128)(2,1)} add(bf16[144,3072]{1,0:T(8,128)(2,1)} %get-tuple-element.105, bf16[144,3072]{1,0:T(8,128)(2,1)S(1)} %collective-permute-done.5) | non-fusion elementwise | flops 442368 | bytes 2654208 | tf_op jit(solution)/shard_map/add | solution.py:740
  71.6 1.8 collective-permute-start.8
  73.4 15.8 %middle_second.1 = (bf16[576,1024]{1,0:T(8,128)(2,1)}, f32[576,1024]{1,0:T(8,128)}, bf16[576,1024]{1,0:T(8,128)(2,1)}, bf16[144,2112]{1,0:T(8,128)(2,1)}, bf16[1...) custom-call(s32[2]{0:T(128)} %pad_add_fusion.ids, bf16[576,1024]{1,0:T(8,128)(2,1)} %bitcast.25, ...), custom_call_target="tpu_custom_call" | custom-call | flops 17999998976 | bytes 1048576 | tf_op jit(solution)/shard_map/middle_second/pallas_call | solution.py:762
  89.2 0.6 collective-permute-start.10
  89.8 1.9 %collective-permute-done.10 = bf16[144,2112]{1,0:T(8,128)(2,1)S(1)} collective-permute-done((bf16[144,2112]{1,0:T(8,128)(2,1)}, bf16[144,2112]{1,0:T(8,128)(2,1)S(1)}, u32[]{:S(2)}, u32[]{:S(2)}) %collective-permute-start.10) | collective-permute-done | bytes 608288 | tf_op jit(solution)/shard_map/ppermute | solution.py:581
  91.7 1.2 add.106
  92.9 0.3 collective-permute-start.13
  93.2 0.2 collective-permute-start.12
  93.4 0.1 collective-permute-done.8
  93.6 0.1 add_add_fusion
  93.8 1.8 collective-permute-start.9
  95.6 8.0 %attend_back.3 = (bf16[320,1024]{1,0:T(8,128)(2,1)}, bf16[4,144,320]{2,1,0:T(8,128)(2,1)}) custom-call(s32[2]{0:T(128)} %pad_add_fusion.ids, s32[4]{0:T(128)} %fusion.1.need, s32[1,1024]{1,0:T(1,128)} %bitcast.21, bf16[576,1024]{1,0:T(8,128)(2,1)} %get-tuple-element.96.q, bf16[192,1024]{1,0:T(8,128)(2,1)} %get-tuple-element.97.k, ...), custom_call_target="tpu_custom_call" | custom-call | flops 8999999488 | bytes 1048576 | tf_op jit(solution)/shard_map/attend_back/pallas_call | solution.py:793
  103.6 5.8 %collective-permute-done.13 = bf16[144,2112]{1,0:T(8,128)(2,1)S(1)} collective-permute-done((bf16[144,2112]{1,0:T(8,128)(2,1)S(1)}, bf16[144,2112]{1,0:T(8,128)(2,1)S(1)}, u32[]{:S(2)}, u32[]{:S(2)}) %collective-permute-start.13) | collective-permute-done | bytes 608288 | tf_op jit(solution)/shard_map/ppermute | solution.py:578
  109.4 0.1 add_add_fusion.1
  109.6 1.5 collective-permute-start.15
  111.3 1.7 collective-permute-start.11
  113.0 8.2 %attend_back.4 = (bf16[320,1024]{1,0:T(8,128)(2,1)}, bf16[4,144,320]{2,1,0:T(8,128)(2,1)}) custom-call(s32[2]{0:T(128)} %pad_add_fusion.ids, s32[4]{0:T(128)} %fusion.1.need, s32[1,1024]{1,0:T(1,128)} %bitcast.22, bf16[576,1024]{1,0:T(8,128)(2,1)} %get-tuple-element.96.q, bf16[192,1024]{1,0:T(8,128)(2,1)} %get-tuple-element.97.k, ...), custom_call_target="tpu_custom_call" | custom-call | flops 8999999488 | bytes 1048576 | tf_op jit(solution)/shard_map/attend_back/pallas_call | solution.py:793
  121.3 0.8 collective-permute-start.16
  122.2 2.4 %collective-permute-start.14 = (bf16[72,1536]{1,0:T(8,128)(2,1)S(1)}, bf16[72,1536]{1,0:T(8,128)(2,1)S(1)}, u32[]{:S(2)}, u32[]{:S(2)}) collective-permute-start(bf16[72,1536]{1,0:T(8,128)(2,1)S(1)} %dynamic-slice_add_fusion.2), channel_id=1, source_target_pairs={{0,16},{2,18},{4,20},{6,22},{8,24},{10,26},{12,28},{14,30},{16,0},... | collective-permute-start | bytes 663560 | tf_op jit(solution)/shard_map/ppermute | solution.py:581
  124.5 8.9 %attend_back.5 = (bf16[320,1024]{1,0:T(8,128)(2,1)}, bf16[144,960]{1,0:T(8,128)(2,1)}, bf16[144,960]{1,0:T(8,128)(2,1)}, bf16[144,960]{1,0:T(8,128)(2,1)}, bf16[144,960]{1,0:T(8,128)(2,1)}) custom-call(s32[2]{0:T(128)} %pad_add_fusion.ids, s32[4]{0:T(128)} %fusion.1.need, s32[1,1024]{1,0:T(1,128)} %bitcast.23, bf16[576,1024]{1,0:T(8,128)(2,1)} %get-tuple-element.96.q, ...), custom_call_target="tpu_custom_call" | custom-call | flops 8999999488 | bytes 1048576 | tf_op jit(solution)/shard_map/attend_back/pallas_call | solution.py:793
  133.5 1.4 collective-permute-done.14
  135.1 4.1 %collective-permute-start.25 = (bf16[72,1536]{1,0:T(8,128)(2,1)S(1)}, bf16[72,1536]{1,0:T(8,128)(2,1)S(1)}, u32[]{:S(2)}, u32[]{:S(2)}) collective-permute-start(bf16[72,1536]{1,0:T(8,128)(2,1)S(1)} %add.116), channel_id=1, source_target_pairs={{0,8},{2,10},{4,12},{6,14},{8,0},{10,2},{12,4},{14,6},{16,24},{18,... | collective-permute-start | bytes 663560 | tf_op jit(solution)/shard_map/ppermute | solution.py:581
  139.5 6.9 %input_grad.1 = f32[576,1024]{1,0:T(8,128)} custom-call(bf16[576,1024]{1,0:T(8,128)(2,1)} %bitcast.28, f32[576,1024]{1,0:T(8,128)} %get-tuple-element.119.d_mid, bf16[576,960]{1,0:T(8,128)(2,1)} %get-tuple-element.147.w_full, f32[576,8]{1,0:T(8,128)} %get-tuple-element.104.gains, bf16[320,1024]{1,0:T(8,128)(2,1)} %get-tuple-element.127.d_0, ...), custom_call_target="tpu_custom_call" | custom-call | flops 7000000000 | bytes 1048576 | tf_op jit(solution)/shard_map/input_grad/pallas_call | solution.py:820
  146.4 1.8 collective-permute-done.19
  148.4 0.4 collective-permute-start.29
  148.8 4.7 %collective-permute-done.20 = bf16[72,960]{1,0:T(8,128)(2,1)S(1)} collective-permute-done((bf16[72,960]{1,0:T(8,128)(2,1)S(1)}, bf16[72,960]{1,0:T(8,128)(2,1)S(1)}, u32[]{:S(2)}, u32[]{:S(2)}) %collective-permute-start.20) | collective-permute-done | bytes 138272 | tf_op jit(solution)/shard_map/ppermute | solution.py:581
  153.5 0.4 collective-permute-start.21
  153.9 0.1 maximum_select_fusion.2
  154.0 0.3 collective-permute-start.26
  154.3 4.4 %collective-permute-done.21 = bf16[72,960]{1,0:T(8,128)(2,1)S(1)} collective-permute-done((bf16[72,960]{1,0:T(8,128)(2,1)S(1)}, bf16[72,960]{1,0:T(8,128)(2,1)S(1)}, u32[]{:S(2)}, u32[]{:S(2)}) %collective-permute-start.21) | collective-permute-done | bytes 138272 | tf_op jit(solution)/shard_map/ppermute | solution.py:581
  158.8 0.6 collective-permute-start.22
  159.4 0.2 maximum_select_fusion.3
  159.6 0.4 collective-permute-start.30
  159.9 6.3 %collective-permute-done.22 = bf16[72,960]{1,0:T(8,128)(2,1)S(1)} collective-permute-done((bf16[72,960]{1,0:T(8,128)(2,1)S(1)}, bf16[72,960]{1,0:T(8,128)(2,1)S(1)}, u32[]{:S(2)}, u32[]{:S(2)}) %collective-permute-start.22) | collective-permute-done | bytes 138272 | tf_op jit(solution)/shard_map/ppermute | solution.py:581
  166.2 0.7 collective-permute-start.23
  167.0 0.2 collective-permute-done.26
  167.2 0.2 maximum_select_fusion.mine_1
  167.5 6.5 %collective-permute-done.23 = bf16[72,960]{1,0:T(8,128)(2,1)S(1)} collective-permute-done((bf16[72,960]{1,0:T(8,128)(2,1)S(1)}, bf16[72,960]{1,0:T(8,128)(2,1)S(1)}, u32[]{:S(2)}, u32[]{:S(2)}) %collective-permute-start.23) | collective-permute-done | bytes 138272 | tf_op jit(solution)/shard_map/ppermute | solution.py:581
  174.2 0.5 collective-permute-start.24
  174.7 1.7 collective-permute-done.31.got_2
  176.4 0.8 copy-done.11
  177.3 5.5 %finish_hidden.1 = (f32[288,1536]{1,0:T(8,128)}, f32[288,1536]{1,0:T(8,128)}, f32[576,768]{1,0:T(8,128)}, f32[288,576]{1,0:T(8,128)}, f32[288]{0:T(512)}) custom-call(s32[2]{0:T(128)} %pad_add_fusion.ids, bf16[144,3072]{1,0:T(8,128)(2,1)} %copy-done.1, bf16[144,3072]{1,0:T(8,128)(2,1)} %collective-permute-done.27.got_1, bf16[144,2112]{1,0:T(8,128)(2,1)} %copy-done.3, ...), custom_call_target="tpu_custom_call" | custom-call | flops 5000000000 | bytes 1048576 | tf_op jit(solution)/shard_map/finish_hidden/pallas_call | solution.py:845
  182.8 2.6 %finish_last.1 = (f32[288,576]{1,0:T(8,128)}, f32[288,192]{1,0:T(8,128)}, f32[288,192]{1,0:T(8,128)}, f32[288]{0:T(512)}) custom-call(s32[2]{0:T(128)} %pad_add_fusion.ids, bf16[144,960]{1,0:T(8,128)(2,1)} %copy-done.5, bf16[144,960]{1,0:T(8,128)(2,1)} %collective-permute-done.24.got, bf16[288,576]{1,0:T(8,128)(2,1)} %wq.5, bf16[288,192]{1,0:T(8,128)(2,1)} %wk.5, ...), custom_call_target="tpu_custom_call" | custom-call | flops 3000000000 | bytes 1048576 | tf_op jit(solution)/shard_map/finish_last/pallas_call | solution.py:860
  (82 shorter events, 1.8 us)
Async XLA Ops:
  0.6 4.9 %copy-start.16 = (s32[1,4]{1,0:T(1,128)S(1)}, s32[1,4]{1,0:T(1,128)}, u32[]{:S(2)}) copy-start(s32[1,4]{1,0:T(1,128)} %param.14) | copy-start | bytes 52
  2.6 10.9 %collective-permute-start.1 = (bf16[160,960]{1,0:T(8,128)(2,1)}, bf16[160,960]{1,0:T(8,128)(2,1)S(1)}, u32[]{:S(2)}, u32[]{:S(2)}) collective-permute-start(bf16[160,960]{1,0:T(8,128)(2,1)} %pack_first.1.packed), channel_id=1, source_target_pairs={{0,1},{1,0},{2,3},{3,2},{4,5},{5,4},{6,7},{7,6},{8,9},{9,8},{10,11... | collective-permute-start | bytes 921608 | tf_op jit(solution)/shard_map/ppermute | solution.py:578
  5.8 5.8 %copy-start.7 = (s32[1024]{0:T(1024)}, s32[1024]{0:T(1024)S(1)}, u32[]{:S(2)}) copy-start(s32[1024]{0:T(1024)S(1)} %select_reduce_fusion) | copy-start | bytes 12292
  13.4 1.8 copy-start.13
  13.5 1.8 collective-permute-start.2
  13.5 27.0 %collective-permute-start = (bf16[144,3840]{1,0:T(8,128)(2,1)}, bf16[144,3840]{1,0:T(8,128)(2,1)S(1)}, u32[]{:S(2)}, u32[]{:S(2)}) collective-permute-start(bf16[144,3840]{1,0:T(8,128)(2,1)} %get-tuple-element.93), channel_id=1, source_target_pairs={{0,1},{1,0},{2,3},{3,2},{4,5},{5,4},{6,7},{7,6},{8,9},{9,8},{10,11... | collective-permute-start | bytes 3317768 | tf_op jit(solution)/shard_map/ppermute | solution.py:578
  15.2 0.7 copy-start.14
  22.1 18.4 %copy-start.12 = (bf16[144,1536]{1,0:T(8,128)(2,1)S(1)}, bf16[144,1536]{1,0:T(8,128)(2,1)}, u32[]{:S(2)}) copy-start(bf16[144,1536]{1,0:T(8,128)(2,1)} %get-tuple-element.101) | copy-start | bytes 1327108
  40.5 3.7 %copy-start.8 = (bf16[144,3840]{1,0:T(8,128)(2,1)}, bf16[144,3840]{1,0:T(8,128)(2,1)S(1)}, u32[]{:S(2)}) copy-start(bf16[144,3840]{1,0:T(8,128)(2,1)S(1)} %collective-permute-done.wo_a.got_a) | copy-start | bytes 3317764
  40.5 2.7 %collective-permute-start.3 = (bf16[144,3840]{1,0:T(8,128)(2,1)S(1)}, bf16[144,3840]{1,0:T(8,128)(2,1)S(1)}, u32[]{:S(2)}, u32[]{:S(2)}) collective-permute-start(bf16[144,3840]{1,0:T(8,128)(2,1)S(1)} %collective-permute-done.wo_a.got_a), channel_id=1, source_target_pairs={{0,2},{2,0},{4,6},{6,4},{8,10},{10,8},{12,14},{14,12},{16,18},{18,... | collective-permute-start | bytes 3317768 | tf_op jit(solution)/shard_map/ppermute | solution.py:581
  40.5 26.1 %collective-permute-start.4 = (bf16[144,1536]{1,0:T(8,128)(2,1)S(1)}, bf16[144,1536]{1,0:T(8,128)(2,1)}, u32[]{:S(2)}, u32[]{:S(2)}) collective-permute-start(bf16[144,1536]{1,0:T(8,128)(2,1)S(1)} %copy-done.12), channel_id=1, source_target_pairs={{0,1},{1,0},{2,3},{3,2},{4,5},{5,4},{6,7},{7,6},{8,9},{9,8},{10,11... | collective-permute-start | bytes 1327112 | tf_op jit(solution)/shard_map/ppermute | solution.py:578
  43.2 1.0 copy-start.9
  66.6 2.7 %collective-permute-start.5 = (bf16[144,3072]{1,0:T(8,128)(2,1)}, bf16[144,3072]{1,0:T(8,128)(2,1)S(1)}, u32[]{:S(2)}, u32[]{:S(2)}) collective-permute-start(bf16[144,3072]{1,0:T(8,128)(2,1)} %get-tuple-element.109), channel_id=1, source_target_pairs={{0,2},{2,0},{4,6},{6,4},{8,10},{10,8},{12,14},{14,12},{16,18},{18,... | collective-permute-start | bytes 2654216 | tf_op jit(solution)/shard_map/ppermute | solution.py:581
  66.8 6.6 %collective-permute-start.6 = (bf16[144,1536]{1,0:T(8,128)(2,1)}, bf16[144,1536]{1,0:T(8,128)(2,1)}, u32[]{:S(2)}, u32[]{:S(2)}) collective-permute-start(bf16[144,1536]{1,0:T(8,128)(2,1)} %collective-permute-done.4.got_a), channel_id=1, source_target_pairs={{0,2},{2,0},{4,6},{6,4},{8,10},{10,8},{12,14},{14,12},{16,18},{18,... | collective-permute-start | bytes 1327112 | tf_op jit(solution)/shard_map/ppermute | solution.py:581
  71.6 21.9 %collective-permute-start.8 = (bf16[144,3072]{1,0:T(8,128)(2,1)}, bf16[144,3072]{1,0:T(8,128)(2,1)S(1)}, u32[]{:S(2)}, u32[]{:S(2)}) collective-permute-start(bf16[144,3072]{1,0:T(8,128)(2,1)} %add.100), channel_id=1, source_target_pairs={{0,1},{1,0},{2,3},{3,2},{4,5},{5,4},{6,7},{7,6},{8,9},{9,8},{10,11... | collective-permute-start | bytes 2654216 | tf_op jit(solution)/shard_map/ppermute | solution.py:578
  73.4 20.2 %collective-permute-start.7 = (bf16[144,3072]{1,0:T(8,128)(2,1)}, bf16[144,3072]{1,0:T(8,128)(2,1)S(1)}, u32[]{:S(2)}, u32[]{:S(2)}) collective-permute-start(bf16[144,3072]{1,0:T(8,128)(2,1)} %get-tuple-element.118), channel_id=1, source_target_pairs={{0,2},{2,0},{4,6},{6,4},{8,10},{10,8},{12,14},{14,12},{16,18},{18,... | collective-permute-start | bytes 2654216 | tf_op jit(solution)/shard_map/ppermute | solution.py:581
  89.2 4.4 %copy-start = (bf16[144,3072]{1,0:T(8,128)(2,1)S(1)}, bf16[144,3072]{1,0:T(8,128)(2,1)}, u32[]{:S(2)}) copy-start(bf16[144,3072]{1,0:T(8,128)(2,1)} %get-tuple-element.116) | copy-start | bytes 2654212
  89.2 2.5 %collective-permute-start.10 = (bf16[144,2112]{1,0:T(8,128)(2,1)}, bf16[144,2112]{1,0:T(8,128)(2,1)S(1)}, u32[]{:S(2)}, u32[]{:S(2)}) collective-permute-start(bf16[144,2112]{1,0:T(8,128)(2,1)} %get-tuple-element.122), channel_id=1, source_target_pairs={{0,2},{2,0},{4,6},{6,4},{8,10},{10,8},{12,14},{14,12},{16,18},{18,... | collective-permute-start | bytes 1824776 | tf_op jit(solution)/shard_map/ppermute | solution.py:581
  89.8 3.4 %copy-start.10 = (bf16[144,2112]{1,0:T(8,128)(2,1)S(1)}, bf16[144,2112]{1,0:T(8,128)(2,1)}, u32[]{:S(2)}) copy-start(bf16[144,2112]{1,0:T(8,128)(2,1)} %get-tuple-element.131) | copy-start | bytes 1824772
  92.9 16.5 %collective-permute-start.13 = (bf16[144,2112]{1,0:T(8,128)(2,1)S(1)}, bf16[144,2112]{1,0:T(8,128)(2,1)S(1)}, u32[]{:S(2)}, u32[]{:S(2)}) collective-permute-start(bf16[144,2112]{1,0:T(8,128)(2,1)S(1)} %add.106), channel_id=1, source_target_pairs={{0,1},{1,0},{2,3},{3,2},{4,5},{5,4},{6,7},{7,6},{8,9},{9,8},{10,11... | collective-permute-start | bytes 1824776 | tf_op jit(solution)/shard_map/ppermute | solution.py:578
  93.2 16.1 %collective-permute-start.12 = (bf16[144,2112]{1,0:T(8,128)(2,1)S(1)}, bf16[144,2112]{1,0:T(8,128)(2,1)S(1)}, u32[]{:S(2)}, u32[]{:S(2)}) collective-permute-start(bf16[144,2112]{1,0:T(8,128)(2,1)S(1)} %copy-done.10), channel_id=1, source_target_pairs={{0,2},{2,0},{4,6},{6,4},{8,10},{10,8},{12,14},{14,12},{16,18},{18,... | collective-permute-start | bytes 1824776 | tf_op jit(solution)/shard_map/ppermute | solution.py:581
  93.8 17.3 %collective-permute-start.9 = (bf16[72,3072]{1,0:T(8,128)(2,1)S(1)}, bf16[72,3072]{1,0:T(8,128)(2,1)S(1)}, u32[]{:S(2)}, u32[]{:S(2)}) collective-permute-start(bf16[72,3072]{1,0:T(8,128)(2,1)S(1)} %constant_dynamic-slice_fusion.4), channel_id=1, source_target_pairs={{0,4},{2,6},{4,0},{6,2},{8,12},{10,14},{12,8},{14,10},{16,20},{18,... | collective-permute-start | bytes 1327112 | tf_op jit(solution)/shard_map/ppermute | solution.py:581
  95.6 13.8 %copy-start.2 = (bf16[144,2112]{1,0:T(8,128)(2,1)S(1)}, bf16[144,2112]{1,0:T(8,128)(2,1)}, u32[]{:S(2)}) copy-start(bf16[144,2112]{1,0:T(8,128)(2,1)} %get-tuple-element.129) | copy-start | bytes 1824772
  109.6 11.5 %collective-permute-start.15 = (bf16[72,2112]{1,0:T(8,128)(2,1)S(1)}, bf16[72,2112]{1,0:T(8,128)(2,1)S(1)}, u32[]{:S(2)}, u32[]{:S(2)}) collective-permute-start(bf16[72,2112]{1,0:T(8,128)(2,1)S(1)} %constant_dynamic-slice_fusion.2), channel_id=1, source_target_pairs={{0,4},{2,6},{4,0},{6,2},{8,12},{10,14},{12,8},{14,10},{16,20},{18,... | collective-permute-start | bytes 912392 | tf_op jit(solution)/shard_map/ppermute | solution.py:581
  111.3 10.8 %collective-permute-start.11 = (bf16[72,1536]{1,0:T(8,128)(2,1)S(1)}, bf16[72,1536]{1,0:T(8,128)(2,1)S(1)}, u32[]{:S(2)}, u32[]{:S(2)}) collective-permute-start(bf16[72,1536]{1,0:T(8,128)(2,1)S(1)} %constant_dynamic-slice_fusion.3), channel_id=1, source_target_pairs={{0,8},{2,10},{4,12},{6,14},{8,0},{10,2},{12,4},{14,6},{16,24},{18,... | collective-permute-start | bytes 663560 | tf_op jit(solution)/shard_map/ppermute | solution.py:581
  121.3 12.1 %collective-permute-start.16 = (bf16[72,1056]{1,0:T(8,128)(2,1)S(1)}, bf16[72,1056]{1,0:T(8,128)(2,1)S(1)}, u32[]{:S(2)}, u32[]{:S(2)}) collective-permute-start(bf16[72,1056]{1,0:T(8,128)(2,1)S(1)} %constant_dynamic-slice_fusion.1), channel_id=1, source_target_pairs={{0,8},{2,10},{4,12},{6,14},{8,0},{10,2},{12,4},{14,6},{16,24},{18,... | collective-permute-start | bytes 456200 | tf_op jit(solution)/shard_map/ppermute | solution.py:581
  122.2 12.8 %collective-permute-start.14 = (bf16[72,1536]{1,0:T(8,128)(2,1)S(1)}, bf16[72,1536]{1,0:T(8,128)(2,1)S(1)}, u32[]{:S(2)}, u32[]{:S(2)}) collective-permute-start(bf16[72,1536]{1,0:T(8,128)(2,1)S(1)} %dynamic-slice_add_fusion.2), channel_id=1, source_target_pairs={{0,16},{2,18},{4,20},{6,22},{8,24},{10,26},{12,28},{14,30},{16,0},... | collective-permute-start | bytes 663560 | tf_op jit(solution)/shard_map/ppermute | solution.py:581
  133.4 5.9 %copy-start.4 = (bf16[144,960]{1,0:T(8,128)(2,1)S(1)}, bf16[144,960]{1,0:T(8,128)(2,1)}, u32[]{:S(2)}) copy-start(bf16[144,960]{1,0:T(8,128)(2,1)} %get-tuple-element.143) | copy-start | bytes 829444
  133.4 6.0 %copy-start.15 = (bf16[144,960]{1,0:T(8,128)(2,1)S(1)}, bf16[144,960]{1,0:T(8,128)(2,1)}, u32[]{:S(2)}) copy-start(bf16[144,960]{1,0:T(8,128)(2,1)} %get-tuple-element.150) | copy-start | bytes 829444
  135.0 4.3 %collective-permute-start.17 = (bf16[144,960]{1,0:T(8,128)(2,1)}, bf16[144,960]{1,0:T(8,128)(2,1)S(1)}, u32[]{:S(2)}, u32[]{:S(2)}) collective-permute-start(bf16[144,960]{1,0:T(8,128)(2,1)} %get-tuple-element.145), channel_id=1, source_target_pairs={{0,2},{2,0},{4,6},{6,4},{8,10},{10,8},{12,14},{14,12},{16,18},{18,... | collective-permute-start | bytes 829448 | tf_op jit(solution)/shard_map/ppermute | solution.py:581
  135.1 13.3 %collective-permute-start.28 = (bf16[72,1056]{1,0:T(8,128)(2,1)S(1)}, bf16[72,1056]{1,0:T(8,128)(2,1)S(1)}, u32[]{:S(2)}, u32[]{:S(2)}) collective-permute-start(bf16[72,1056]{1,0:T(8,128)(2,1)S(1)} %dynamic-slice_add_fusion.3), channel_id=1, source_target_pairs={{0,16},{2,18},{4,20},{6,22},{8,24},{10,26},{12,28},{14,30},{16,0},... | collective-permute-start | bytes 456200 | tf_op jit(solution)/shard_map/ppermute | solution.py:581
  135.1 13.6 %collective-permute-start.25 = (bf16[72,1536]{1,0:T(8,128)(2,1)S(1)}, bf16[72,1536]{1,0:T(8,128)(2,1)S(1)}, u32[]{:S(2)}, u32[]{:S(2)}) collective-permute-start(bf16[72,1536]{1,0:T(8,128)(2,1)S(1)} %add.116), channel_id=1, source_target_pairs={{0,8},{2,10},{4,12},{6,14},{8,0},{10,2},{12,4},{14,6},{16,24},{18,... | collective-permute-start | bytes 663560 | tf_op jit(solution)/shard_map/ppermute | solution.py:581
  139.3 8.9 %collective-permute-start.19 = (bf16[144,960]{1,0:T(8,128)(2,1)S(1)}, bf16[144,960]{1,0:T(8,128)(2,1)S(1)}, u32[]{:S(2)}, u32[]{:S(2)}) collective-permute-start(bf16[144,960]{1,0:T(8,128)(2,1)S(1)} %add.119), channel_id=1, source_target_pairs={{0,1},{1,0},{2,3},{3,2},{4,5},{5,4},{6,7},{7,6},{8,9},{9,8},{10,11... | collective-permute-start | bytes 829448 | tf_op jit(solution)/shard_map/ppermute | solution.py:578
  139.4 8.8 %collective-permute-start.18 = (bf16[144,960]{1,0:T(8,128)(2,1)S(1)}, bf16[144,960]{1,0:T(8,128)(2,1)S(1)}, u32[]{:S(2)}, u32[]{:S(2)}) collective-permute-start(bf16[144,960]{1,0:T(8,128)(2,1)S(1)} %copy-done.15), channel_id=1, source_target_pairs={{0,2},{2,0},{4,6},{6,4},{8,10},{10,8},{12,14},{14,12},{16,18},{18,... | collective-permute-start | bytes 829448 | tf_op jit(solution)/shard_map/ppermute | solution.py:581
  139.5 8.7 %copy-start.6 = (bf16[144,960]{1,0:T(8,128)(2,1)S(1)}, bf16[144,960]{1,0:T(8,128)(2,1)}, u32[]{:S(2)}) copy-start(bf16[144,960]{1,0:T(8,128)(2,1)} %get-tuple-element.148) | copy-start | bytes 829444
  148.3 5.2 %collective-permute-start.20 = (bf16[72,960]{1,0:T(8,128)(2,1)S(1)}, bf16[72,960]{1,0:T(8,128)(2,1)S(1)}, u32[]{:S(2)}, u32[]{:S(2)}) collective-permute-start(bf16[72,960]{1,0:T(8,128)(2,1)S(1)} %constant_dynamic-slice_fusion), channel_id=1, source_target_pairs={{0,4},{2,6},{4,0},{6,2},{8,12},{10,14},{12,8},{14,10},{16,20},{18,... | collective-permute-start | bytes 414728 | tf_op jit(solution)/shard_map/ppermute | solution.py:581
  148.4 5.9 %collective-permute-start.29 = (bf16[72,1056]{1,0:T(8,128)(2,1)S(1)}, bf16[72,1056]{1,0:T(8,128)(2,1)S(1)}, u32[]{:S(2)}, u32[]{:S(2)}) collective-permute-start(bf16[72,1056]{1,0:T(8,128)(2,1)S(1)} %add.125), channel_id=1, source_target_pairs={{0,8},{2,10},{4,12},{6,14},{8,0},{10,2},{12,4},{14,6},{16,24},{18,... | collective-permute-start | bytes 456200 | tf_op jit(solution)/shard_map/ppermute | solution.py:581
  153.5 5.2 %collective-permute-start.21 = (bf16[72,960]{1,0:T(8,128)(2,1)S(1)}, bf16[72,960]{1,0:T(8,128)(2,1)S(1)}, u32[]{:S(2)}, u32[]{:S(2)}) collective-permute-start(bf16[72,960]{1,0:T(8,128)(2,1)S(1)} %dynamic-slice_add_fusion.4), channel_id=1, source_target_pairs={{0,8},{2,10},{4,12},{6,14},{8,0},{10,2},{12,4},{14,6},{16,24},{18,... | collective-permute-start | bytes 414728 | tf_op jit(solution)/shard_map/ppermute | solution.py:581
  154.0 13.2 %collective-permute-start.26 = (bf16[72,3072]{1,0:T(8,128)(2,1)S(1)}, bf16[72,3072]{1,0:T(8,128)(2,1)S(1)}, u32[]{:S(2)}, u32[]{:S(2)}) collective-permute-start(bf16[72,3072]{1,0:T(8,128)(2,1)S(1)} %maximum_select_fusion.2), channel_id=1, source_target_pairs={{0,4},{2,6},{4,0},{6,2},{8,12},{10,14},{12,8},{14,10},{16,20},{18,... | collective-permute-start | bytes 1327112 | tf_op jit(solution)/shard_map/ppermute | solution.py:581
  158.8 7.4 %collective-permute-start.22 = (bf16[72,960]{1,0:T(8,128)(2,1)S(1)}, bf16[72,960]{1,0:T(8,128)(2,1)S(1)}, u32[]{:S(2)}, u32[]{:S(2)}) collective-permute-start(bf16[72,960]{1,0:T(8,128)(2,1)S(1)} %add.123), channel_id=1, source_target_pairs={{0,16},{2,18},{4,20},{6,22},{8,24},{10,26},{12,28},{14,30},{16,0},... | collective-permute-start | bytes 414728 | tf_op jit(solution)/shard_map/ppermute | solution.py:581
  159.6 14.4 %collective-permute-start.30 = (bf16[72,2112]{1,0:T(8,128)(2,1)S(1)}, bf16[72,2112]{1,0:T(8,128)(2,1)S(1)}, u32[]{:S(2)}, u32[]{:S(2)}) collective-permute-start(bf16[72,2112]{1,0:T(8,128)(2,1)S(1)} %maximum_select_fusion.3), channel_id=1, source_target_pairs={{0,4},{2,6},{4,0},{6,2},{8,12},{10,14},{12,8},{14,10},{16,20},{18,... | collective-permute-start | bytes 912392 | tf_op jit(solution)/shard_map/ppermute | solution.py:581
  166.2 7.7 %collective-permute-start.23 = (bf16[72,960]{1,0:T(8,128)(2,1)S(1)}, bf16[72,960]{1,0:T(8,128)(2,1)S(1)}, u32[]{:S(2)}, u32[]{:S(2)}) collective-permute-start(bf16[72,960]{1,0:T(8,128)(2,1)S(1)} %add.124), channel_id=1, source_target_pairs={{0,4},{2,6},{4,0},{6,2},{8,12},{10,14},{12,8},{14,10},{16,20},{18,... | collective-permute-start | bytes 414728 | tf_op jit(solution)/shard_map/ppermute | solution.py:581
  167.4 9.9 %copy-start.1 = (bf16[144,3072]{1,0:T(8,128)(2,1)}, bf16[144,3072]{1,0:T(8,128)(2,1)S(1)}, u32[]{:S(2)}) copy-start(bf16[144,3072]{1,0:T(8,128)(2,1)S(1)} %maximum_select_fusion.mine_1) | copy-start | bytes 2654212
  167.4 9.8 %collective-permute-start.27 = (bf16[144,3072]{1,0:T(8,128)(2,1)S(1)}, bf16[144,3072]{1,0:T(8,128)(2,1)}, u32[]{:S(2)}, u32[]{:S(2)}) collective-permute-start(bf16[144,3072]{1,0:T(8,128)(2,1)S(1)} %maximum_select_fusion.mine_1), channel_id=1, source_target_pairs={{0,2},{2,0},{4,6},{6,4},{8,10},{10,8},{12,14},{14,12},{16,18},{18,... | collective-permute-start | bytes 2654216 | tf_op jit(solution)/shard_map/ppermute | solution.py:581
  174.0 8.8 %copy-start.5 = (bf16[144,960]{1,0:T(8,128)(2,1)}, bf16[144,960]{1,0:T(8,128)(2,1)S(1)}, u32[]{:S(2)}) copy-start(bf16[144,960]{1,0:T(8,128)(2,1)S(1)} %maximum_select_fusion.4.mine) | copy-start | bytes 829444
  174.2 3.1 %copy-start.3 = (bf16[144,2112]{1,0:T(8,128)(2,1)}, bf16[144,2112]{1,0:T(8,128)(2,1)S(1)}, u32[]{:S(2)}) copy-start(bf16[144,2112]{1,0:T(8,128)(2,1)S(1)} %maximum_select_fusion.1.mine_2) | copy-start | bytes 1824772
  174.2 2.2 %collective-permute-start.31 = (bf16[144,2112]{1,0:T(8,128)(2,1)S(1)}, bf16[144,2112]{1,0:T(8,128)(2,1)S(1)}, u32[]{:S(2)}, u32[]{:S(2)}) collective-permute-start(bf16[144,2112]{1,0:T(8,128)(2,1)S(1)} %maximum_select_fusion.1.mine_2), channel_id=1, source_target_pairs={{0,2},{2,0},{4,6},{6,4},{8,10},{10,8},{12,14},{14,12},{16,18},{18,... | collective-permute-start | bytes 1824776 | tf_op jit(solution)/shard_map/ppermute | solution.py:581
  174.2 8.6 %collective-permute-start.24 = (bf16[144,960]{1,0:T(8,128)(2,1)S(1)}, bf16[144,960]{1,0:T(8,128)(2,1)}, u32[]{:S(2)}, u32[]{:S(2)}) collective-permute-start(bf16[144,960]{1,0:T(8,128)(2,1)S(1)} %maximum_select_fusion.4.mine), channel_id=1, source_target_pairs={{0,2},{2,0},{4,6},{6,4},{8,10},{10,8},{12,14},{14,12},{16,18},{18,... | collective-permute-start | bytes 829448 | tf_op jit(solution)/shard_map/ppermute | solution.py:581
  176.4 0.8 copy-start.11
